TPU v7x, 512 devices: a whole 4x4x16 slice. The times are simulated.
512 devices in a mesh: ctx: 64 (over z, x_hi, core), tp: 8 (over y, x_lo).
Axes of the slice: x: 4 (x_hi: 2, x_lo: 2; x = x_hi * 2 + x_lo), y: 4, z: 16, core: 2. Of those that a mesh axis runs over, the one named last changes fastest.
Arguments:
- pre_q: bfloat16 [8192, 8192], P('ctx', 'tp'), may hold values from -90 to 90
- pre_k: bfloat16 [8192, 1024], P('ctx', 'tp'), may hold values from -4.5 to 4.5
- pre_v: bfloat16 [8192, 1024], P('ctx', 'tp'), may hold values from -6 to 6
- page_table: int32 [64, 96], P('ctx'), may hold values from 0 to 511, as said below
- dec_q: bfloat16 [256, 4, 8192], P('ctx', None, 'tp'), may hold values from -90 to 90
- dec_new_k: bfloat16 [256, 4, 1024], P('ctx', None, 'tp'), may hold values from -4.5 to 4.5
- dec_new_v: bfloat16 [256, 4, 1024], P('ctx', None, 'tp'), may hold values from -6 to 6
- cache_k: bfloat16 [256, 512, 1024], P('ctx', None, 'tp'), may hold values from -6 to 6
- cache_v: bfloat16 [256, 512, 1024], P('ctx', None, 'tp'), may hold values from -6 to 6
- cache_len: int32 [256], P('ctx'), may hold values from 1 to 512
- out_weight: bfloat16 [8192, 8192], P('tp', 'ctx'), may hold values from -3 to 3
Outputs:
- pre_out: bfloat16 [8192, 8192], P('ctx', 'tp')
- dec_out: bfloat16 [1024, 8192], P('tp', 'ctx')
Inputs may be any that keep to these rules, and one draw needn't show every extreme that they name: `page_table`: each owner's row names at least one and at most 2 pages of every index of ctx (whose pages are 8 p to 8 p + 7 for index p), and no page twice.
All inputs are finite; a program needn't handle non-finite values.
Results may differ from a plain program's by a relative error of at most 0.019.
Values may be sent and summed in bfloat16 or wider, within the bound.
A program may use at most 64 MiB of HBM per device.

v0:
```python
import jax
import jax.numpy as jnp
from jax import lax
from jax.sharding import PartitionSpec as P

QH = 64
KVH = 8
HD = 128
CACHE = 512
PAGE = 16
MOST = 2
STEPS = 4


NEGATIVE = -1e30


def block_length(length):
    for candidate in (512, 256, 128):
        return candidate
    return length


def attend_step(state, queries, positions, key_block, value_block, key_start):
    score_scale = HD ** (-0.5)

    def compute(current):
        run_max, run_sum, run_acc = current
        scores = (
            jnp.einsum("nkgd,jkd->nkgj", queries, key_block, preferred_element_type=jnp.float32)
            * score_scale
        )
        key_pos = key_start + jnp.arange(key_block.shape[0], dtype=jnp.int32)
        live_mask = (key_pos[None, :] <= positions[:, None])[:, None, None, :]
        scores = jnp.where(live_mask, scores, NEGATIVE)
        new_max = jnp.maximum(run_max, jnp.max(scores, axis=-1))
        factor = jnp.exp(run_max - new_max)
        weights = jnp.where(live_mask, jnp.exp(scores - new_max[..., None]), 0.0)
        new_sum = run_sum * factor + jnp.sum(weights, axis=-1)
        new_acc = run_acc * factor[..., None] + jnp.einsum(
            "nkgj,jkd->nkgd",
            weights.astype(jnp.bfloat16),
            value_block,
            preferred_element_type=jnp.float32,
        )
        return (new_max, new_sum, new_acc)

    return lax.cond(key_start > jnp.max(positions), lambda current: current, compute, state)


def local(
    pre_q,
    pre_k,
    pre_v,
    page_table,
    dec_q,
    dec_new_k,
    dec_new_v,
    cache_k,
    cache_v,
    cache_len,
    out_weight,
):
    group_size = QH // KVH
    score_scale = HD ** (-0.5)
    token_count = pre_q.shape[0]
    key_local = pre_k.shape[1]
    kv_local = key_local // HD
    query_local = pre_q.shape[1]
    ctx_count = lax.axis_size("ctx")
    ctx_index = lax.axis_index("ctx")
    queries = pre_q.reshape(token_count, kv_local, group_size, HD)
    own_positions = ctx_index * token_count + jnp.arange(token_count, dtype=jnp.int32)
    groups = ((queries, own_positions),)
    slot_pages = page_table[0]
    slot_total = slot_pages.shape[0]
    states_init = tuple(
        (
            (
                jnp.full((member[0].shape[0], kv_local, group_size), NEGATIVE, jnp.float32),
                jnp.zeros((member[0].shape[0], kv_local, group_size), jnp.float32),
                jnp.zeros((member[0].shape[0], kv_local, group_size, HD), jnp.float32),
            )
            for member in groups
        )
    )
    key_piece = lax.all_gather(pre_k, "ctx", axis=0, tiled=True)
    value_piece = lax.all_gather(pre_v, "ctx", axis=0, tiled=True)
    length = key_piece.shape[0]
    block_span = block_length(length)
    block_count = length // block_span
    key_blocks = key_piece.reshape(block_count, block_span, kv_local, HD)
    value_blocks = value_piece.reshape(block_count, block_span, kv_local, HD)
    offsets = block_span * jnp.arange(block_count, dtype=jnp.int32)

    def scan_step(inner_states, block_items):
        key_block, value_block, offset = block_items
        updated = tuple(
            (
                attend_step(
                    inner_states[number],
                    groups[number][0],
                    groups[number][1],
                    key_block,
                    value_block,
                    offset,
                )
                for number in range(len(groups))
            )
        )
        return (updated, None)

    states, _ = lax.scan(scan_step, states_init, (key_blocks, value_blocks, offsets))
    outputs = [
        (member[2] / member[1][..., None]).astype(jnp.bfloat16).reshape(-1, query_local)
        for member in states
    ]
    pre_out = outputs[0]
    page_count = token_count // PAGE
    local_pages = jnp.concatenate([pre_k, pre_v], axis=1).reshape(page_count, PAGE * 2 * key_local)
    source = slot_pages // page_count
    within = slot_pages % page_count
    slot_ids = jnp.arange(slot_total, dtype=jnp.int32)
    same_source = (source[None, :] == source[:, None]) & (slot_ids[None, :] < slot_ids[:, None])
    slot_rank = jnp.sum(same_source.astype(jnp.int32), axis=1)
    device_ids = jnp.arange(ctx_count, dtype=jnp.int32)
    depth_ids = jnp.arange(MOST, dtype=jnp.int32)
    matches = (source[:, None, None] == device_ids[None, :, None]) & (
        slot_rank[:, None, None] == depth_ids[None, None, :]
    )
    requests = jnp.sum(jnp.where(matches, within[:, None, None] + 1, 0), axis=0) - 1
    selector = (
        lax.all_to_all(requests, "ctx", split_axis=0, concat_axis=0, tiled=True)[..., None]
        == jnp.arange(page_count, dtype=jnp.int32)
    ).astype(jnp.bfloat16)
    packed = jnp.einsum(
        "nmp,pf->nmf", selector, local_pages, preferred_element_type=jnp.float32
    ).astype(jnp.bfloat16)
    arrived = lax.all_to_all(packed, "ctx", split_axis=0, concat_axis=0, tiled=True)
    chooser = matches.reshape(slot_total, ctx_count * MOST).astype(jnp.bfloat16)
    pool_all = jnp.dot(
        chooser,
        arrived.reshape(ctx_count * MOST, PAGE * 2 * key_local),
        preferred_element_type=jnp.float32,
    ).astype(jnp.bfloat16)
    pool_flat = pool_all.reshape(slot_total * PAGE, 2 * key_local)
    pool_keys = pool_flat[:, :key_local].reshape(slot_total * PAGE, kv_local, HD)
    pool_values = pool_flat[:, key_local:].reshape(slot_total * PAGE, kv_local, HD)
    row_local = dec_q.shape[0]
    dec_queries = dec_q.reshape(row_local, STEPS, kv_local, group_size, HD)
    cache_keys = cache_k.reshape(row_local, CACHE, kv_local, HD)
    cache_values = cache_v.reshape(row_local, CACHE, kv_local, HD)
    new_keys = dec_new_k.reshape(row_local, STEPS, kv_local, HD)
    new_values = dec_new_v.reshape(row_local, STEPS, kv_local, HD)
    pool_scores = (
        jnp.einsum("rtkgd,jkd->rtkgj", dec_queries, pool_keys, preferred_element_type=jnp.float32)
        * score_scale
    )
    cache_scores = (
        jnp.einsum("rtkgd,rjkd->rtkgj", dec_queries, cache_keys, preferred_element_type=jnp.float32)
        * score_scale
    )
    new_scores = (
        jnp.einsum("rtkgd,rjkd->rtkgj", dec_queries, new_keys, preferred_element_type=jnp.float32)
        * score_scale
    )
    cache_live = (jnp.arange(CACHE, dtype=jnp.int32)[None, :] < cache_len[:, None])[
        :, None, None, None, :
    ]
    step_ids = jnp.arange(STEPS, dtype=jnp.int32)
    new_live = (step_ids[None, :] <= step_ids[:, None])[None, :, None, None, :]
    cache_scores = jnp.where(cache_live, cache_scores, NEGATIVE)
    new_scores = jnp.where(new_live, new_scores, NEGATIVE)
    top_score = jnp.maximum(
        jnp.maximum(jnp.max(pool_scores, axis=-1), jnp.max(cache_scores, axis=-1)),
        jnp.max(new_scores, axis=-1),
    )[..., None]
    pool_weights = jnp.exp(pool_scores - top_score)
    cache_weights = jnp.where(cache_live, jnp.exp(cache_scores - top_score), 0.0)
    new_weights = jnp.where(new_live, jnp.exp(new_scores - top_score), 0.0)
    totals = (
        jnp.sum(pool_weights, axis=-1)
        + jnp.sum(cache_weights, axis=-1)
        + jnp.sum(new_weights, axis=-1)
    )
    mixed = jnp.einsum(
        "rtkgj,jkd->rtkgd",
        pool_weights.astype(jnp.bfloat16),
        pool_values,
        preferred_element_type=jnp.float32,
    )
    mixed = mixed + jnp.einsum(
        "rtkgj,rjkd->rtkgd",
        cache_weights.astype(jnp.bfloat16),
        cache_values,
        preferred_element_type=jnp.float32,
    )
    mixed = mixed + jnp.einsum(
        "rtkgj,rjkd->rtkgd",
        new_weights.astype(jnp.bfloat16),
        new_values,
        preferred_element_type=jnp.float32,
    )
    attention = (
        (mixed / totals[..., None]).astype(jnp.bfloat16).reshape(row_local * STEPS, query_local)
    )
    partial_terms = jnp.dot(
        lax.all_gather(attention, "ctx", axis=0, tiled=True),
        out_weight,
        preferred_element_type=jnp.float32,
    )
    dec_out = lax.psum_scatter(
        partial_terms.astype(jnp.bfloat16), "tp", scatter_dimension=0, tiled=True
    )
    return (pre_out, dec_out)


def solution(mesh):
    placed = (
        P("ctx", "tp"),
        P("ctx", "tp"),
        P("ctx", "tp"),
        P("ctx", None),
        P("ctx", None, "tp"),
        P("ctx", None, "tp"),
        P("ctx", None, "tp"),
        P("ctx", None, "tp"),
        P("ctx", None, "tp"),
        P("ctx"),
        P("tp", "ctx"),
    )
    return jax.shard_map(
        local,
        mesh=mesh,
        in_specs=placed,
        out_specs=(P("ctx", "tp"), P("tp", "ctx")),
        check_vma=False,
    )
```

profile of v0, /device:TPU:481, one launch (start us, length us, event | category | flops | bytes accessed | tf_op | source)
XLA Modules:
  0.0 612.8 jit_solution(14872953003848754229)
XLA Ops:
  7.2 0.7 and_select_fusion.3
  8.9 0.7 copy.36
  9.6 12.5 %all-to-all-start = ((s32[64,1,2]{2,1,0:T(1,128)}), s32[64,1,2]{2,1,0:T(1,128)S(1)}, u32[]{:S(2)}, u32[]{:S(2)}) async-start(s32[64,1,2]{2,1,0:T(1,128)} %copy.36), calls=%async_computation | async-start | bytes 65536 | tf_op jit(solution)/shard_map/all_to_all | solution.py:133
  22.1 0.8 pad_maximum_fusion
  22.9 10.9 %all-to-all-done = s32[64,1,2]{2,1,0:T(1,128)S(1)} async-done(((s32[64,1,2]{2,1,0:T(1,128)}), s32[64,1,2]{2,1,0:T(1,128)S(1)}, u32[]{:S(2)}, u32[]{:S(2)}) %all-to-all-start) | async-done | bytes 544 | tf_op jit(solution)/shard_map/all_to_all | solution.py:133
  34.4 2.1 copy.38
  36.5 7.8 %all-to-all-start.1 = ((bf16[64,2,4096]{2,1,0:T(2,128)(2,1)}), bf16[64,2,4096]{2,1,0:T(2,128)(2,1)S(1)}, u32[]{:S(2)}, u32[]{:S(2)}) async-start(bf16[64,2,4096]{2,1,0:T(2,128)(2,1)} %copy.38), calls=%async_computation.1 | async-start | bytes 2097152 | tf_op jit(solution)/shard_map/all_to_all | solution.py:139
  45.1 49.7 %all-to-all-done.1 = bf16[64,2,4096]{2,1,0:T(2,128)(2,1)S(1)} async-done(((bf16[64,2,4096]{2,1,0:T(2,128)(2,1)}), bf16[64,2,4096]{2,1,0:T(2,128)(2,1)S(1)}, u32[]{:S(2)}, u32[]{:S(2)}) %all-to-all-start.1) | async-done | bytes 1048608 | tf_op jit(solution)/shard_map/all_to_all | solution.py:139
  94.8 1.3 fusion.25
  100.5 138.2 %all-gather.8.cloned.1.call-done = bf16[1024,1024]{1,0:T(8,128)(2,1)} async-done(((bf16[16,1024]{1,0:T(8,128)(2,1)}), bf16[1024,1024]{1,0:T(8,128)(2,1)}) %all-gather.8.cloned.1.call-update) | async-done | bytes 2097168 | tf_op jit(solution)/shard_map/all_gather | solution.py:208
  238.7 3.0 convolution_convert_fusion.1
  242.8 137.4 %all-gather.6.cloned.1.call-done = bf16[8192,128]{1,0:T(8,128)(2,1)} async-done(((bf16[128,128]{1,0:T(8,128)(2,1)}), bf16[8192,128]{1,0:T(8,128)(2,1)}) %all-gather.6.cloned.1.call-update) | async-done | bytes 2097168 | tf_op jit(solution)/shard_map/all_gather | solution.py:88
  380.2 2.9 copy.34
  383.0 138.7 %all-gather.4.cloned.1.call-done = bf16[8192,128]{1,0:T(8,128)(2,1)} async-done(((bf16[128,128]{1,0:T(8,128)(2,1)}), bf16[8192,128]{1,0:T(8,128)(2,1)}) %all-gather.4.cloned.1.call-update) | async-done | bytes 2097168 | tf_op jit(solution)/shard_map/all_gather | solution.py:87
  521.8 83.6 %while.16 = (s32[]{:T(128)}, f32[128,1,8]{0,2,1:T(8,128)S(1)}, f32[128,1,8]{0,2,1:T(8,128)S(1)}, f32[128,1,8,128]{0,3,2,1:T(8,128)S(1)}, s32[16]{0:T(128)S(1)}, ...) while((s32[]{:T(128)}, f32[128,1,8]{0,2,1:T(8,128)S(1)}, ...), condition=%wide.region_6.7_spmd.clone, body=%wide.region_1.6_spmd.clone.sunk | while | flops 275582592 | bytes 8198939 | solution.py:113
  523.6 3.4 conditional.3
  524.3 1.4 fusion.2
  526.2 0.7 fusion.5
  528.8 3.4 conditional.3
  529.5 1.4 fusion.2
  531.5 0.7 fusion.5
  534.0 3.4 conditional.3
  534.8 1.4 fusion.2
  536.7 0.7 fusion.5
  539.2 3.4 conditional.3
  540.0 1.4 fusion.2
  541.9 0.7 fusion.5
  544.5 3.4 conditional.3
  545.2 1.4 fusion.2
  547.1 0.7 fusion.5
  549.7 3.4 conditional.3
  550.4 1.4 fusion.2
  552.3 0.7 fusion.5
  554.9 3.4 conditional.3
  555.7 1.4 fusion.2
  557.6 0.7 fusion.5
  560.1 3.4 conditional.3
  560.9 1.4 fusion.2
  562.8 0.7 fusion.5
  565.4 3.4 conditional.3
  566.1 1.4 fusion.2
  568.0 0.7 fusion.5
  570.6 3.4 conditional.3
  571.3 1.4 fusion.2
  573.2 0.7 fusion.5
  575.8 3.4 conditional.3
  576.5 1.4 fusion.2
  578.5 0.7 fusion.5
  581.0 3.4 conditional.3
  581.8 1.4 fusion.2
  583.7 0.7 fusion.5
  586.2 3.4 conditional.3
  587.0 1.4 fusion.2
  588.9 0.7 fusion.5
  591.5 3.4 conditional.3
  592.2 1.4 fusion.2
  594.1 0.7 fusion.5
  596.7 3.4 conditional.3
  597.4 1.4 fusion.2
  599.4 0.7 fusion.5
  601.9 3.4 conditional.3
  602.7 1.4 fusion.2
  604.6 0.7 fusion.5
  605.4 0.9 copy.47
  (202 shorter events, 37.0 us)
Async XLA Ops:
  7.2 37.6 %copy-start = (bf16[4,512,128]{2,1,0:T(8,128)(2,1)S(1)}, bf16[4,512,128]{2,1,0:T(8,128)(2,1)}, u32[]{:S(2)}) copy-start(bf16[4,512,128]{2,1,0:T(8,128)(2,1)} %param.22) | copy-start | bytes 1572868
  9.6 24.2 %all-to-all-start = ((s32[64,1,2]{2,1,0:T(1,128)}), s32[64,1,2]{2,1,0:T(1,128)S(1)}, u32[]{:S(2)}, u32[]{:S(2)}) async-start(s32[64,1,2]{2,1,0:T(1,128)} %copy.36), calls=%async_computation | async-start | bytes 65536 | tf_op jit(solution)/shard_map/all_to_all | solution.py:133
  34.4 10.0 %copy-start.3 = (bf16[4,4,1024]{2,1,0:T(4,128)(2,1)S(1)}, bf16[4,4,1024]{2,1,0:T(4,128)(2,1)}, u32[]{:S(2)}) copy-start(bf16[4,4,1024]{2,1,0:T(4,128)(2,1)} %param.19) | copy-start | bytes 98308
  34.4 10.0 %copy-start.5 = (s32[4]{0:T(128)S(1)}, s32[4]{0:T(128)}, u32[]{:S(2)}) copy-start(s32[4]{0:T(128)} %param.24) | copy-start | bytes 52
  34.4 10.1 %copy-start.7 = (bf16[4,4,128]{2,1,0:T(4,128)(2,1)S(1)}, bf16[4,4,128]{2,1,0:T(4,128)(2,1)}, u32[]{:S(2)}) copy-start(bf16[4,4,128]{2,1,0:T(4,128)(2,1)} %param.20) | copy-start | bytes 12292
  36.5 58.3 %all-to-all-start.1 = ((bf16[64,2,4096]{2,1,0:T(2,128)(2,1)}), bf16[64,2,4096]{2,1,0:T(2,128)(2,1)S(1)}, u32[]{:S(2)}, u32[]{:S(2)}) async-start(bf16[64,2,4096]{2,1,0:T(2,128)(2,1)} %copy.38), calls=%async_computation.1 | async-start | bytes 2097152 | tf_op jit(solution)/shard_map/all_to_all | solution.py:139
  44.3 194.5 %all-gather.8.cloned.1.call-start = ((), (), s32[]{:S(2)}) async-start(), calls=%async_computation.5 | async-start | bytes 2129920 | tf_op jit(solution)/shard_map/all_gather | solution.py:208
  96.8 0.7 copy-start.4
  96.8 1.2 copy-start.6
  96.9 141.9 %copy-start.1 = (bf16[1024,128]{1,0:T(8,128)(2,1)S(1)}, bf16[1024,128]{1,0:T(8,128)(2,1)}, u32[]{:S(2)}) copy-start(bf16[1024,128]{1,0:T(8,128)(2,1)} %param.25) | copy-start | bytes 786436
  98.0 144.4 %copy-start.2 = (bf16[128,1024]{1,0:T(8,128)(2,1)S(1)}, bf16[128,1024]{1,0:T(8,128)(2,1)}, u32[]{:S(2)}) copy-start(bf16[128,1024]{1,0:T(8,128)(2,1)} %param.15) | copy-start | bytes 786436
  99.0 281.2 %all-gather.6.cloned.1.call-start = ((), (), s32[]{:S(2)}) async-start(), calls=%async_computation.4 | async-start | bytes 2129920 | tf_op jit(solution)/shard_map/all_gather | solution.py:88
  99.7 422.0 %all-gather.4.cloned.1.call-start = ((), (), s32[]{:S(2)}) async-start(), calls=%async_computation.3 | async-start | bytes 2129920 | tf_op jit(solution)/shard_map/all_gather | solution.py:87
  100.5 505.8 %reduce-scatter.2.cloned.1.call-start = ((), (), s32[]{:S(2)}) async-start(), calls=%async_computation.6 | async-start | bytes 294912 | tf_op jit(solution)/shard_map/reduce_scatter | solution.py:212
Sparse Core Ops, SparseCore 0:
  99.1 139.5 all-gather.7
  242.0 138.1 all-gather.5
  383.5 138.2 all-gather.3
  525.0 35.9 reduce-scatter.1
where the time goes:
time: 614 us; the launch traced here: 613 us
  waiting for transfers between devices  476 us (78%)
  matrix products  40.3 us (7%)
  other arithmetic  23.8 us (4%)
  loops' own time  20.7 us (3%)
  starting transfers between devices  20.4 us (3%)
  local copies, waits for them, and re-layouts  17.4 us (3%)
  between operations  14 us (2%)
    all_gather x1, waiting for transfers between devices, local(): key_piece = lax.all_gather(pre_k, 'ctx', axis=0, tiled=True)  139 us
    all_gather x1, waiting for transfers between devices, local(): lax.all_gather(attention, 'ctx', axis=0, tiled=True)  138 us
    all_gather x1, waiting for transfers between devices, local(): value_piece = lax.all_gather(pre_v, 'ctx', axis=0, tiled=True)  137 us
    all_to_all x1, waiting for transfers between devices, local(): lax.all_to_all(packed, 'ctx', split_axis=0, concat_axis=0, tiled=True)  49.7 us
    dot_general x16, matrix products, compute(): jnp.einsum('nkgd,jkd->nkgj', queries, key_block, preferred_element_type=j...  21.8 us
    another operation x1, loops' own time, local(): lax.scan(scan_step, states_init, (key_blocks, value_blocks, offsets))  19.5 us
    all_to_all x1, starting transfers between devices, local(): lax.all_to_all(requests, 'ctx', split_axis=0, concat_axis=0, tiled=True)  12.5 us
  transfers between devices with their start and end apart: 6, of which 5 were waited for; matrix products, arithmetic and copies ran while one was open for 12% of the time, Pallas kernels for 0%

commit v1 on v0

v1 whole, which is shorter than its diff:
```python
import functools
import math

import jax
import jax.numpy as jnp
from jax import lax
from jax.experimental import pallas as pl
from jax.experimental.pallas import tpu as pltpu
from jax.sharding import PartitionSpec as P

MESH = pl.DeviceIdType.MESH
HD = 128
GROUP = 8
PAGE = 16
STEPS = 4
NEGATIVE = -1e30
SCALE = HD ** -0.5 * math.log2(math.e)
F32 = jnp.float32
BF16 = jnp.bfloat16


def dot_t(a, b):
    return lax.dot_general(a, b, (((1,), (1,)), ((), ())), preferred_element_type=F32)


def dot(a, b):
    return jnp.dot(a, b, preferred_element_type=F32)


def wide(a, n):
    return jnp.concatenate([a] * n, axis=1)


def with_ones(values):
    return jnp.concatenate([values, jnp.ones(values.shape, BF16)], axis=1)


def row_max(scores):
    top = jnp.max(scores, axis=1, keepdims=True)
    return jnp.broadcast_to(top, (scores.shape[0], HD))


def kernel(
    nz, ntp,
    q_hbm, k_hbm, v_hbm, table, dq_ref, nk_ref, nv_ref, ck_hbm, cv_hbm, lens, w_hbm,
    pre_hbm, dec_hbm,
    kv, qv, ck, cv, wv, acc, top, dq32, nk32, nv32, dacc, dtop, pool_k, pool_v,
    att, sbuf, rbuf, prev, decv,
    loc, zs, zr, ss, sr, os, orr, xs, xr, ws, wr, at_s, at_r, rs, rr,
):
    half = nz // 2
    plane = ntp * 4
    ctx = lax.axis_index("ctx")
    tp = lax.axis_index("tp")
    z, xh, c = ctx // 4, (ctx // 2) % 2, ctx % 2
    mine = ctx % 4
    slots = table.shape[1]

    def device(zz, xx, cc):
        return (zz * 4 + xx * 2 + cc, tp)

    def move(src, dst, send, recv, to):
        return pltpu.make_async_remote_copy(
            src_ref=src, dst_ref=dst, send_sem=send, recv_sem=recv, device_id=to, device_id_type=MESH
        )

    sibling = device(z, xh, 1 - c)
    beside = device(z, 1 - xh, c)
    across = device(z, 1 - xh, 1 - c)

    def toward(d):
        return device(lax.rem(z + (1 if d == 0 else nz - 1), nz), xh, c)

    def block(d, s):
        return lax.rem(jnp.where(d == 0, z + nz - s, z + s), nz)

    def side(p):
        return xh if p == 0 else 1 - xh

    loads = [
        pltpu.make_async_copy(k_hbm, kv.at[z, c, xh, 0], loc.at[0]),
        pltpu.make_async_copy(v_hbm, kv.at[z, c, xh, 1], loc.at[1]),
        pltpu.make_async_copy(w_hbm, wv.at[xh, c], loc.at[2]),
        pltpu.make_async_copy(q_hbm, qv, loc.at[3]),
        pltpu.make_async_copy(ck_hbm, ck, loc.at[4]),
        pltpu.make_async_copy(cv_hbm, cv, loc.at[5]),
    ]
    for load in loads:
        load.start()
    barrier = pltpu.get_barrier_semaphore()
    here = tp * 4 + mine

    def greet(o, _):
        to = lax.rem(here + o, plane)
        pl.semaphore_signal(barrier, inc=1, device_id=(z * 4 + to % 4, to // 4), device_id_type=MESH)
        return 0

    for d in (0, 1):
        pl.semaphore_signal(barrier, inc=1, device_id=toward(d), device_id_type=MESH)
    lax.fori_loop(1, plane, greet, 0)
    loads[0].wait()
    loads[1].wait()
    pl.semaphore_wait(barrier, plane + 1)

    def along(d, p, s, zb):
        ref = kv.at[zb, c, side(p)]
        return move(ref, ref, zs.at[d, p, s - 1], zr.at[d, p, s - 1], toward(d))

    def over(d, p, s, cc):
        ref = kv.at[block(d, s), cc, side(p)]
        return move(ref, ref, ss.at[d, p, s - 1], sr.at[d, p, s - 1], sibling)

    def over_own(p, cc):
        ref = kv.at[z, cc, side(p)]
        return move(ref, ref, os.at[p], orr.at[p], sibling)

    def swap(p):
        ref = kv.at[z, c, side(p)]
        return move(ref, ref, xs, xr, beside)

    peers = ((sibling, xh, 1 - c), (beside, 1 - xh, c), (across, 1 - xh, 1 - c))

    def weight(n, xx, cc):
        ref = wv.at[xx, cc]
        return move(ref, ref, ws.at[n], wr.at[n], peers[n][0])

    def sends(p, d):
        return half > 1 or p == d

    swap(0).start()
    for d in (0, 1):
        if sends(0, d):
            along(d, 0, 1, z).start()
    over_own(0, c).start()
    swap(1).wait_recv()
    for d in (0, 1):
        if sends(1, d):
            along(d, 1, 1, z).start()
    over_own(1, c).start()
    loads[2].wait()
    for n in range(3):
        weight(n, xh, c).start()
    for load in loads[3:]:
        load.wait()

    for r in range(4):
        dq32[pl.ds(r * STEPS, STEPS), :] = dq_ref[r].astype(F32)
    nk32[...] = jnp.zeros_like(nk32)
    nv32[...] = jnp.zeros_like(nv32)
    for r in range(4):
        nk32[pl.ds(r * STEPS, STEPS), :] = nk_ref[r].astype(F32)
        nv32[pl.ds(r * STEPS, STEPS), :] = nv_ref[r].astype(F32)

    def decode_queries():
        rows = dq32[...].astype(BF16)
        return jnp.concatenate([rows[:, h * HD:(h + 1) * HD] for h in range(GROUP)], axis=0)

    queries = decode_queries()
    rows = queries.shape[0]

    def own_decode():
        cache = ck.shape[1]
        q_id = lax.broadcasted_iota(jnp.int32, (rows, cache), 0)
        k_id = lax.broadcasted_iota(jnp.int32, (rows, cache), 1)
        q_row = (q_id >> 2) & 3
        scores = []
        for r in range(4):
            live = (q_row == r) & (k_id < lens[r])
            scores.append(jnp.where(live, dot_t(queries, ck[r]), NEGATIVE))
        n_id = lax.broadcasted_iota(jnp.int32, (rows, HD), 0)
        u_id = lax.broadcasted_iota(jnp.int32, (rows, HD), 1)
        live = ((u_id >> 2) == ((n_id >> 2) & 3)) & ((u_id & 3) <= (n_id & 3))
        scores.append(jnp.where(live, dot_t(queries, nk32[...].astype(BF16)), NEGATIVE))
        most = row_max(scores[-1])
        for r in range(4):
            most = jnp.maximum(most, row_max(scores[r]))
        total = jnp.zeros((rows, 2 * HD), F32)
        for r in range(4):
            weights = jnp.exp2((scores[r] - wide(most, cache // HD)) * SCALE)
            total += dot(weights.astype(BF16), with_ones(cv[r]))
        weights = jnp.exp2((scores[-1] - most) * SCALE)
        total += dot(weights.astype(BF16), with_ones(nv32[...].astype(BF16)))
        dacc[...] = total
        dtop[...] = most

    own_decode()

    order = ((0, 0), (0, 1), (1, 0), (1, 1))
    tokens = qv.shape[0]
    span = 4 * tokens

    def attend(zb, masked):
        keys = jnp.concatenate([kv[zb, cc, xx, 0].reshape(tokens, HD) for cc, xx in order], axis=0)
        values = with_ones(
            jnp.concatenate([kv[zb, cc, xx, 1].reshape(tokens, HD) for cc, xx in order], axis=0)
        )
        live = None
        if masked:
            q_id = lax.broadcasted_iota(jnp.int32, (2 * tokens, span), 0) & (tokens - 1)
            k_id = lax.broadcasted_iota(jnp.int32, (2 * tokens, span), 1)
            place = k_id // tokens
            place = (place & 1) * 2 + (place >> 1)
            live = place * tokens + (k_id & (tokens - 1)) <= mine * tokens + q_id
        for pair in range(GROUP // 2):
            first = 2 * pair * HD
            q2 = jnp.concatenate([qv[:, first:first + HD], qv[:, first + HD:first + 2 * HD]], axis=0)
            scores = dot_t(q2, keys)
            if masked:
                scores = jnp.where(live, scores, NEGATIVE)
                most = row_max(scores)
            else:
                old = top[pair]
                most = jnp.maximum(old, row_max(scores))
            weights = jnp.exp2((scores - wide(most, span // HD)) * SCALE)
            mixed = dot(weights.astype(BF16), values)
            if not masked:
                mixed += acc[pair] * wide(jnp.exp2((old - most) * SCALE), 2)
            acc[pair] = mixed
            top[pair] = most

    for p in (0, 1):
        over_own(p, 1 - c).wait_recv()
    attend(z, True)

    def attend_step(d, s):
        needed = jnp.where(d == 0, z - s >= 0, z + s >= nz)

        @pl.when(needed)
        def _():
            attend(block(d, s), False)

    def wait_over(s, pieces):
        for p, d in pieces:
            over(d, p, s, 1 - c).wait_recv()

    every = [(p, d) for p in (0, 1) for d in (0, 1)]
    last = [(0, 0), (1, 1)]

    def ring(s, _):
        for p, d in every:
            zb = block(d, s)
            along(d, p, s, zb).wait_recv()
            if p == d:
                along(d, p, s + 1, zb).start()
            else:
                @pl.when(s < half - 1)
                def _():
                    along(d, p, s + 1, zb).start()
            over(d, p, s, c).start()

        @pl.when(s > 1)
        def _():
            wait_over(s - 1, every)

            def both(d, _):
                attend_step(d, s - 1)
                return 0

            lax.fori_loop(0, 2, both, 0)

        return 0

    lax.fori_loop(1, half, ring, 0)
    for p, d in last:
        along(d, p, half, block(d, half)).wait_recv()
        over(d, p, half, c).start()
    if half > 1:
        wait_over(half - 1, every)
    wait_over(half, last)

    def fetch(slot, _):
        page = table[0, slot]
        zz, xx, cc, at = page >> 5, (page >> 4) & 1, (page >> 3) & 1, page & 7
        pool_k[slot] = kv[zz, cc, xx, 0, at]
        pool_v[slot] = kv[zz, cc, xx, 1, at]
        return 0

    lax.fori_loop(0, slots, fetch, 0, unroll=8)
    scores = dot_t(queries, pool_k[...].reshape(slots * PAGE, HD))
    most = jnp.maximum(dtop[...], row_max(scores))
    weights = jnp.exp2((scores - wide(most, slots * PAGE // HD)) * SCALE)
    total = dot(weights.astype(BF16), with_ones(pool_v[...].reshape(slots * PAGE, HD)))
    total += dacc[...] * wide(jnp.exp2((dtop[...] - most) * SCALE), 2)
    mixed = (total[:, :HD] / total[:, HD:]).astype(BF16)
    lines = rows // GROUP
    for h in range(GROUP):
        att[z, h // 4, h % 4] = mixed[h * lines:(h + 1) * lines]

    def share(d, s, zb):
        return move(att.at[zb], att.at[zb], at_s.at[d, s - 1], at_r.at[d, s - 1], toward(d))

    def share_half(d, zb):
        ref = att.at[zb, d]
        return move(ref, ref, at_s.at[d, half - 1], at_r.at[d, half - 1], toward(d))

    for d in (0, 1):
        if half > 1:
            share(d, 1, z).start()
        else:
            share_half(d, z).start()

    def pass_on(s, _):
        for d in (0, 1):
            zb = block(d, s)
            share(d, s, zb).wait_recv()

            @pl.when(s < half - 1)
            def _():
                share(d, s + 1, zb).start()

            @pl.when(s == half - 1)
            def _():
                share_half(d, zb).start()

        return 0

    lax.fori_loop(1, half, pass_on, 0)
    for n in range(3):
        weight(n, peers[n][1], peers[n][2]).wait_recv()
    for d in (0, 1):
        share_half(d, block(d, half)).wait_recv()

    lhs = jnp.concatenate(
        [att[:, h // 4, h % 4].reshape(nz * lines, HD) for h in range(GROUP)], axis=1
    )
    depth = sbuf.shape[2]
    for xx in (0, 1):
        part = dot(lhs, jnp.concatenate([wv[xx, 0], wv[xx, 1]], axis=1)).astype(BF16)
        for cc in (0, 1):
            for j in range(ntp):
                sbuf[j, xx * 2 + cc] = part[j * depth:(j + 1) * depth, cc * HD:(cc + 1) * HD]

    def deal(o, to, source):
        return move(
            sbuf.at[to // 4, to % 4],
            rbuf.at[source // 4, source % 4],
            rs.at[o - 1],
            rr.at[o - 1],
            (z * 4 + to % 4, to // 4),
        )

    def deal_out(o, _):
        deal(o, lax.rem(here + o, plane), here).start()
        return 0

    lax.fori_loop(1, plane, deal_out, 0)
    rbuf[tp, mine] = sbuf[tp, mine]

    def rest(n, _):
        attend_step(n % 2, half - 1 + n // 2)
        return 0

    lax.fori_loop(0 if half > 1 else 2, 3, rest, 0)
    for pair in range(GROUP // 2):
        total = acc[pair]
        out = (total[:, :HD] / total[:, HD:]).astype(BF16)
        for n in (0, 1):
            first = (2 * pair + n) * HD
            prev[:, first:first + HD] = out[n * tokens:(n + 1) * tokens]
    store_pre = pltpu.make_async_copy(prev, pre_hbm, loc.at[6])
    store_pre.start()

    def deal_in(o, _):
        deal(o, lax.rem(here + o, plane), lax.rem(here + plane - o, plane)).wait_recv()
        return 0

    lax.fori_loop(1, plane, deal_in, 0)
    for n in range(4):
        total = rbuf[0, n].astype(F32)
        for j in range(1, ntp):
            total += rbuf[j, n].astype(F32)
        total = total.astype(BF16)
        for zz in range(depth // lines):
            decv[zz * 4 + n] = total[zz * lines:(zz + 1) * lines]
    store_dec = pltpu.make_async_copy(decv, dec_hbm, loc.at[7])
    store_dec.start()

    def ring_sent(s, _):
        for p, d in every:
            along(d, p, s, block(d, s - 1)).wait_send()
            over(d, p, s, c).wait_send()
        return 0

    lax.fori_loop(1, half, ring_sent, 0)
    for p, d in last:
        along(d, p, half, block(d, half - 1)).wait_send()
        over(d, p, half, c).wait_send()
    swap(0).wait_send()
    for p in (0, 1):
        over_own(p, c).wait_send()
    for n in range(3):
        weight(n, xh, c).wait_send()
    for d in (0, 1):
        def shared(s, _):
            share(d, s, block(d, s - 1)).wait_send()
            return 0

        lax.fori_loop(1, half, shared, 0)
        share_half(d, block(d, half - 1)).wait_send()

    def dealt(o, _):
        deal(o, lax.rem(here + o, plane), here).wait_send()
        return 0

    lax.fori_loop(1, plane, dealt, 0)
    store_pre.wait()
    store_dec.wait()


def local(pre_q, pre_k, pre_v, page_table, dec_q, dec_new_k, dec_new_v, cache_k, cache_v, cache_len, out_weight):
    nz = lax.axis_size("ctx") // 4
    ntp = lax.axis_size("tp")
    half = nz // 2
    tokens = pre_q.shape[0]
    pages = tokens // PAGE
    row_dev, cache = cache_k.shape[:2]
    slots = page_table.shape[1]
    lines = row_dev * STEPS
    plane = 4 * ntp
    out_rows = nz * 4 * lines // ntp
    depth = nz // ntp * lines
    any_space = pl.BlockSpec(memory_space=pl.ANY)
    vmem = pl.BlockSpec(memory_space=pltpu.VMEM)
    smem = pl.BlockSpec(memory_space=pltpu.SMEM)
    sem = pltpu.SemaphoreType.DMA
    pre_out, dec_out = pl.pallas_call(
        functools.partial(kernel, nz, ntp),
        out_shape=(
            jax.ShapeDtypeStruct((tokens, GROUP * HD), BF16),
            jax.ShapeDtypeStruct((out_rows // lines, lines, HD), BF16),
        ),
        in_specs=[
            any_space, any_space, any_space, smem, vmem, vmem, vmem,
            any_space, any_space, smem, any_space,
        ],
        out_specs=(any_space, any_space),
        scratch_shapes=[
            pltpu.VMEM((nz, 2, 2, 2, pages, PAGE, HD), BF16),
            pltpu.VMEM((tokens, GROUP * HD), BF16),
            pltpu.VMEM((row_dev, cache, HD), BF16),
            pltpu.VMEM((row_dev, cache, HD), BF16),
            pltpu.VMEM((2, 2, GROUP * HD, HD), BF16),
            pltpu.VMEM((GROUP // 2, 2 * tokens, 2 * HD), F32),
            pltpu.VMEM((GROUP // 2, 2 * tokens, HD), F32),
            pltpu.VMEM((lines, GROUP * HD), F32),
            pltpu.VMEM((HD, HD), F32),
            pltpu.VMEM((HD, HD), F32),
            pltpu.VMEM((GROUP * lines, 2 * HD), F32),
            pltpu.VMEM((GROUP * lines, HD), F32),
            pltpu.VMEM((slots, PAGE, HD), BF16),
            pltpu.VMEM((slots, PAGE, HD), BF16),
            pltpu.VMEM((nz, 2, 4, lines, HD), BF16),
            pltpu.VMEM((ntp, 4, depth, HD), BF16),
            pltpu.VMEM((ntp, 4, depth, HD), BF16),
            pltpu.VMEM((tokens, GROUP * HD), BF16),
            pltpu.VMEM((out_rows // lines, lines, HD), BF16),
            sem((8,)),
            sem((2, 2, half)), sem((2, 2, half)),
            sem((2, 2, half)), sem((2, 2, half)),
            sem((2,)), sem((2,)),
            sem(()), sem(()),
            sem((3,)), sem((3,)),
            sem((2, half)), sem((2, half)),
            sem((plane - 1,)), sem((plane - 1,)),
        ],
        compiler_params=pltpu.CompilerParams(
            collective_id=0, has_side_effects=True, vmem_limit_bytes=40 << 20
        ),
    )(
        pre_q,
        pre_k.reshape(pages, PAGE, HD),
        pre_v.reshape(pages, PAGE, HD),
        page_table,
        dec_q,
        dec_new_k,
        dec_new_v,
        cache_k,
        cache_v,
        cache_len,
        out_weight,
    )
    return (pre_out, dec_out.reshape(out_rows, HD))


def solution(mesh):
    placed = (
        P("ctx", "tp"),
        P("ctx", "tp"),
        P("ctx", "tp"),
        P("ctx", None),
        P("ctx", None, "tp"),
        P("ctx", None, "tp"),
        P("ctx", None, "tp"),
        P("ctx", None, "tp"),
        P("ctx", None, "tp"),
        P("ctx"),
        P("tp", "ctx"),
    )
    return jax.shard_map(
        local,
        mesh=mesh,
        in_specs=placed,
        out_specs=(P("ctx", "tp"), P("tp", "ctx")),
        check_vma=False,
    )
```

time: 614 us -> 96.5 us (0.16)
  the two profiles are of different devices: /device:TPU:481 before, /device:TPU:1 now
where the time goes in v1:
time: 96.5 us; the launch traced here: 95.9 us
  Pallas kernels  85.7 us (89%)
  local copies, waits for them, and re-layouts  9.6 us (10%)
    pallas_call x1, Pallas kernels, local(): pl.pallas_call(functools.partial(kernel, nz, ntp), out_shape=(jax.ShapeDt...  85.7 us
    unnamed x24, local copies, waits for them, and re-layouts  9.6 us

profile of v1, /device:TPU:1, one launch (start us, length us, event | category | flops | bytes accessed | tf_op | source)
XLA Modules:
  0.0 95.9 jit_solution(14638381494614360048)
XLA Ops:
  0.6 0.0 copy-start.9
  0.6 0.0 copy-start.10
  0.7 0.6 copy-done.9
  1.3 0.0 copy-done.10
  1.3 0.0 copy-start
  1.3 1.0 %copy-done = bf16[4,512,128]{2,1,0:T(8,128)(2,1)S(1)} copy-done((bf16[4,512,128]{2,1,0:T(8,128)(2,1)S(1)}, bf16[4,512,128]{2,1,0:T(8,128)(2,1)}, u32[]{:S(2)}) %copy-start) | copy-done | bytes 524312
  2.3 0.0 copy-start.1
  2.4 1.0 %copy-done.1 = bf16[4,512,128]{2,1,0:T(8,128)(2,1)S(1)} copy-done((bf16[4,512,128]{2,1,0:T(8,128)(2,1)S(1)}, bf16[4,512,128]{2,1,0:T(8,128)(2,1)}, u32[]{:S(2)}) %copy-start.1) | copy-done | bytes 524312
  3.4 0.0 copy-start.2
  3.4 0.9 copy-done.2
  4.3 0.0 copy-start.3
  4.3 0.9 copy-done.3
  5.3 0.0 copy-start.4
  5.3 0.8 copy-done.4
  6.0 0.0 copy-start.5
  6.1 0.8 copy-done.5
  6.8 0.0 copy-start.6
  6.8 0.8 copy-done.6
  7.6 0.0 copy-start.7
  7.6 0.7 copy-done.7
  8.3 0.0 copy-start.8
  8.3 0.7 copy-done.8
  8.9 85.7 %shard_map.122 = (bf16[128,1024]{1,0:T(8,128)(2,1)S(1)}, bf16[8,16,128]{2,1,0:T(8,128)(2,1)S(1)}) custom-call(bf16[128,1024]{1,0:T(8,128)(2,1)S(1)} %copy-done.2, bf16[8,16,128]{2,1,0:T(8,128)(2,1)S(1)} %bitcast.3, bf16[8,16,128]{2,1,0:T(8,128)(2,1)S(1)} %bitcast.4, s32[1,96]{1,0:T(1,128)S(1)} %copy-done.9, bf16[4,4,1024]{2,1,0:T(4,128)(2,1)S(1)} %copy-done.6, ...), custom_call_target="tpu_custom_call" | custom-call | tf_op jit(solution)/shard_map/pallas_call | solution.py:426
  94.6 0.7 copy.15
  95.3 0.6 copy.16
Async XLA Ops:
  0.6 0.7 copy-start.9
  0.6 0.7 copy-start.10
  1.3 1.0 %copy-start = (bf16[4,512,128]{2,1,0:T(8,128)(2,1)S(1)}, bf16[4,512,128]{2,1,0:T(8,128)(2,1)}, u32[]{:S(2)}) copy-start(bf16[4,512,128]{2,1,0:T(8,128)(2,1)} %ck_hbm.1) | copy-start | bytes 1572868
  2.3 1.0 %copy-start.1 = (bf16[4,512,128]{2,1,0:T(8,128)(2,1)S(1)}, bf16[4,512,128]{2,1,0:T(8,128)(2,1)}, u32[]{:S(2)}) copy-start(bf16[4,512,128]{2,1,0:T(8,128)(2,1)} %cv_hbm.1) | copy-start | bytes 1572868
  3.4 0.9 copy-start.2
  4.3 0.9 copy-start.3
  5.3 0.8 copy-start.4
  6.0 0.8 copy-start.5
  6.8 0.8 copy-start.6
  7.6 0.7 copy-start.7
  8.3 0.7 copy-start.8

commit v2 on v1

v2 whole, which is shorter than its diff:
```python
import functools
import math

import jax
import jax.numpy as jnp
from jax import lax
from jax.experimental import pallas as pl
from jax.experimental.pallas import tpu as pltpu
from jax.sharding import PartitionSpec as P

MESH = pl.DeviceIdType.MESH
HD = 128
GROUP = 8
STEPS = 4
NEGATIVE = -1e30
SCALE = HD ** -0.5 * math.log2(math.e)
F32 = jnp.float32
BF16 = jnp.bfloat16


def dot_t(a, b):
    return lax.dot_general(a, b, (((1,), (1,)), ((), ())), preferred_element_type=F32)


def dot(a, b):
    return jnp.dot(a, b, preferred_element_type=F32)


def wide(a, n):
    return jnp.concatenate([a] * n, axis=1)


def with_ones(values):
    return jnp.concatenate([values, jnp.ones(values.shape, BF16)], axis=1)


def row_max(scores):
    top = jnp.max(scores, axis=1, keepdims=True)
    return jnp.broadcast_to(top, (scores.shape[0], HD))


def kernel(
    nz, ntp,
    q_hbm, k_hbm, v_hbm, table_hbm, dq_hbm, nk_hbm, nv_hbm, ck_hbm, cv_hbm, lens_hbm, w_hbm,
    pre_hbm, dec_hbm,
    table, lens, dq_in, nk_in, nv_in,
    kv, qv, ck, cv, wv, acc, top, dq32, nk32, nv32, dqs, flags, bias, dacc, dtop,
    ob, ost, db, dst, att, sbuf, rbuf, prev, decv,
    loc, zs, zr, ss, sr, os, orr, xs, xr, ws, wr, at_s, at_r, rs, rr,
):
    half = nz // 2
    plane = ntp * 4
    ctx = lax.axis_index("ctx")
    tp = lax.axis_index("tp")
    z, xh, c = ctx // 4, (ctx // 2) % 2, ctx % 2
    mine = ctx % 4
    here = tp * 4 + mine
    tokens = qv.shape[1]
    cache = ck.shape[1]
    slots = table.shape[1]
    lines = dq32.shape[0]
    rows = GROUP * lines

    def device(zz, xx, cc):
        return (zz * 4 + xx * 2 + cc, tp)

    def move(src, dst, send, recv, to):
        return pltpu.make_async_remote_copy(
            src_ref=src, dst_ref=dst, send_sem=send, recv_sem=recv, device_id=to, device_id_type=MESH
        )

    sibling = device(z, xh, 1 - c)
    beside = device(z, 1 - xh, c)

    def toward(d):
        return device(lax.rem(z + (1 if d == 0 else nz - 1), nz), xh, c)

    def block(d, s):
        return lax.rem(jnp.where(d == 0, z + nz - s, z + s), nz)

    loads = [
        pltpu.make_async_copy(a, b, loc.at[n])
        for n, (a, b) in enumerate((
            (k_hbm, kv.at[z, c, 0]),
            (v_hbm, kv.at[z, c, 1]),
            (table_hbm, table),
            (dq_hbm, dq_in),
            (nk_hbm, nk_in),
            (nv_hbm, nv_in),
            (lens_hbm, lens),
            (ck_hbm, ck),
            (cv_hbm, cv),
            (q_hbm, qv.at[0]),
            (w_hbm, wv.at[xh, c]),
        ))
    ]
    for load in loads:
        load.start()
    barrier = pltpu.get_barrier_semaphore()

    def greet(o, _):
        to = lax.rem(here + o, plane)
        pl.semaphore_signal(barrier, inc=1, device_id=(z * 4 + to % 4, to // 4), device_id_type=MESH)
        return 0

    for d in (0, 1):
        pl.semaphore_signal(barrier, inc=1, device_id=toward(d), device_id_type=MESH)
    lax.fori_loop(1, plane, greet, 0)
    loads[0].wait()
    loads[1].wait()
    pl.semaphore_wait(barrier, plane + 1)

    def along(d, p, s, zb):
        ref = kv.at[zb, c, p]
        return move(ref, ref, zs.at[d, p, s - 1], zr.at[d, p, s - 1], toward(d))

    def over(d, s, cc):
        ref = kv.at[block(d, s), cc]
        return move(ref, ref, ss.at[d, s - 1], sr.at[d, s - 1], sibling)

    def over_own(cc):
        ref = kv.at[z, cc]
        return move(ref, ref, os, orr, sibling)

    every = [(p, d) for p in (0, 1) for d in (0, 1)]
    for p, d in every:
        along(d, p, 1, z).start()
    over_own(c).start()

    for load in loads[2:4]:
        load.wait()
    for r in range(4):
        dq32[pl.ds(r * STEPS, STEPS), :] = dq_in[r].astype(F32)
    line = dq32[...].astype(BF16)
    for h in range(GROUP):
        dqs[0, h * lines:(h + 1) * lines] = line[:, h * HD:(h + 1) * HD]

    page_row = lax.broadcasted_iota(jnp.int32, flags.shape[1:], 0)
    page_col = lax.broadcasted_iota(jnp.int32, flags.shape[1:], 1)
    page_id = jnp.where(page_col < 32, page_row * 32 + page_col, -1)

    def flag(slot, found):
        return jnp.where(page_id == table[0, slot], 1.0, found)

    flags[0] = lax.fori_loop(0, slots, flag, jnp.zeros(flags.shape[1:], F32), unroll=8)

    def swap(n, src, dst):
        return move(src, dst, xs.at[n], xr.at[n], beside)

    swaps = [
        swap(0, dqs.at[0], dqs.at[1]),
        swap(1, flags.at[0], flags.at[1]),
        swap(2, q_hbm, qv.at[1]),
        swap(3, ob.at[0], ob.at[1]),
        swap(4, ost.at[0], ost.at[1]),
        swap(5, db.at[0], db.at[1]),
        swap(6, dst.at[0], dst.at[1]),
    ]

    def weight(n, xx, source, to):
        return move(source, wv.at[xx, c], ws.at[n], wr.at[n], to)

    weights_out = [
        weight(0, xh, w_hbm, sibling),
        weight(1, xh, w_hbm, beside),
        weight(2, 1 - xh, wv.at[1 - xh, c], sibling),
    ]

    def weight_in(n, xx, cc):
        ref = wv.at[xx, cc]
        return move(ref, ref, ws.at[n], wr.at[n], sibling)

    for n in range(3):
        swaps[n].start()
    for n in range(2):
        weights_out[n].start()

    def own_decode():
        for load in loads[4:9]:
            load.wait()
        nk32[...] = jnp.zeros_like(nk32)
        nv32[...] = jnp.zeros_like(nv32)
        for r in range(4):
            nk32[pl.ds(r * STEPS, STEPS), :] = nk_in[r].astype(F32)
            nv32[pl.ds(r * STEPS, STEPS), :] = nv_in[r].astype(F32)
        queries = dqs[0]
        q_id = lax.broadcasted_iota(jnp.int32, (rows, cache), 0)
        k_id = lax.broadcasted_iota(jnp.int32, (rows, cache), 1)
        q_row = (q_id >> 2) & 3
        scores = []
        for r in range(4):
            live = (q_row == r) & (k_id < lens[r])
            scores.append(jnp.where(live, dot_t(queries, ck[r]), NEGATIVE))
        n_id = lax.broadcasted_iota(jnp.int32, (rows, HD), 0)
        u_id = lax.broadcasted_iota(jnp.int32, (rows, HD), 1)
        live = ((u_id >> 2) == ((n_id >> 2) & 3)) & ((u_id & 3) <= (n_id & 3))
        scores.append(jnp.where(live, dot_t(queries, nk32[...].astype(BF16)), NEGATIVE))
        most = row_max(scores[-1])
        for r in range(4):
            most = jnp.maximum(most, row_max(scores[r]))
        total = jnp.zeros((rows, 2 * HD), F32)
        for r in range(4):
            weights = jnp.exp2((scores[r] - wide(most, cache // HD)) * SCALE)
            total += dot(weights.astype(BF16), with_ones(cv[r]))
        weights = jnp.exp2((scores[-1] - most) * SCALE)
        total += dot(weights.astype(BF16), with_ones(nv32[...].astype(BF16)))
        dacc[0:rows] = total
        dtop[0:rows] = most
        dacc[rows:] = jnp.zeros((rows, 2 * HD), F32)
        dtop[rows:] = jnp.full((rows, HD), NEGATIVE, F32)

    def page_bias():
        span = 2 * tokens
        lane = lax.broadcasted_iota(jnp.int32, (HD, span), 0)
        key = lax.broadcasted_iota(jnp.int32, (HD, span), 1)
        spread = (lane == xh * 16 + (key >> 4)).astype(F32).astype(BF16)
        for n in (0, 1):
            named = dot(flags[n].astype(BF16), spread)
            penalty = jnp.where(named > 0.5, 0.0, NEGATIVE)
            for zz in range(nz):
                bias[n, zz] = jnp.broadcast_to(penalty[zz:zz + 1], (8, span))

    def tall(a, n):
        return jnp.concatenate([a] * n, axis=0)

    def keys_of(blocks):
        return jnp.concatenate([kv[zb, cc, 0] for zb in blocks for cc in (0, 1)], axis=0)

    def values_of(blocks):
        return with_ones(jnp.concatenate([kv[zb, cc, 1] for zb in blocks for cc in (0, 1)], axis=0))

    def decode_step(blocks):
        queries = jnp.concatenate([dqs[0], dqs[1]], axis=0)
        scores = dot_t(queries, keys_of(blocks))
        penalty = jnp.concatenate(
            [
                jnp.concatenate([tall(bias[n, zb], rows // 8) for n in (0, 1)], axis=0)
                for zb in blocks
            ],
            axis=1,
        )
        scores = scores + penalty
        old = dtop[...]
        most = jnp.maximum(old, row_max(scores))
        weights = jnp.exp2((scores - wide(most, scores.shape[1] // HD)) * SCALE)
        dacc[...] = dacc[...] * wide(jnp.exp2((old - most) * SCALE), 2) + dot(
            weights.astype(BF16), values_of(blocks)
        )
        dtop[...] = most

    pairs = GROUP // 2

    def attend(side, zb, masked):
        keys = keys_of([zb])
        values = values_of([zb])
        live = None
        if masked:
            q_id = lax.broadcasted_iota(jnp.int32, (2 * tokens, 2 * tokens), 0) & (tokens - 1)
            k_id = lax.broadcasted_iota(jnp.int32, (2 * tokens, 2 * tokens), 1)
            live = k_id <= c * tokens + q_id
        for pair in range(pairs):
            first = 2 * pair * HD
            q2 = jnp.concatenate(
                [qv[side, :, first:first + HD], qv[side, :, first + HD:first + 2 * HD]], axis=0
            )
            scores = dot_t(q2, keys)
            place = side * pairs + pair
            if masked:
                scores = jnp.where(live, scores, NEGATIVE)
                most = row_max(scores)
            else:
                old = top[place]
                most = jnp.maximum(old, row_max(scores))
            weights = jnp.exp2((scores - wide(most, 2 * tokens // HD)) * SCALE)
            mixed = dot(weights.astype(BF16), values)
            if not masked:
                mixed += acc[place] * wide(jnp.exp2((old - most) * SCALE), 2)
            acc[place] = mixed
            top[place] = most

    def attend_pair(side, s):
        def one(d, _):
            @pl.when(jnp.where(d == 0, z - s >= 0, z + s >= nz))
            def _():
                attend(side, block(d, s), False)

            return 0

        lax.fori_loop(0, 2, one, 0)

    early = 2 if half >= 4 else 0

    def attend_number(n):
        side = jnp.where((n >= early) & (n < early + half - 1), 1, 0)
        s = jnp.where(n < early, n + 1, jnp.where(side == 1, n - early + 1, n - half + 2))
        attend_pair(side, s)

    def ring(s, _):
        for p, d in every:
            zb = block(d, s)
            along(d, p, s, zb).wait_recv()
            if p == d:
                along(d, p, s + 1, zb).start()
            else:
                @pl.when(s < half - 1)
                def _():
                    along(d, p, s + 1, zb).start()
            if p == 1:
                over(d, s, c).start()

        @pl.when(s == 1)
        def _():
            own_decode()
            loads[9].wait()
            over_own(1 - c).wait_recv()
            attend(0, z, True)
            swaps[0].wait_recv()
            swaps[1].wait_recv()
            page_bias()
            decode_step([z])
            acc[pairs:] = jnp.zeros((pairs, 2 * tokens, 2 * HD), F32)
            top[pairs:] = jnp.full((pairs, 2 * tokens, HD), NEGATIVE, F32)

        @pl.when(s > 1)
        def _():
            for d in (0, 1):
                over(d, s - 1, 1 - c).wait_recv()
            decode_step([block(0, s - 1), block(1, s - 1)])

            @pl.when(s == early + 2)
            def _():
                swaps[2].wait_recv()

            attend_number(s - 2)

        return 0

    lax.fori_loop(1, half, ring, 0)
    if half - 1 < early + 2:
        swaps[2].wait_recv()
    for d in (0, 1):
        over(d, half - 1, 1 - c).wait_recv()
    decode_step([block(0, half - 1), block(1, half - 1)])
    weights_out[1].wait_recv()
    weights_out[2].start()
    for d in (0, 1):
        along(d, d, half, block(d, half)).wait_recv()
    over(0, half, c).start()
    over(0, half, 1 - c).wait_recv()
    decode_step([block(0, half)])

    eye = lax.broadcasted_iota(jnp.int32, (HD, HD), 0) == lax.broadcasted_iota(jnp.int32, (HD, HD), 1)

    def flat(a):
        return jnp.sum(jnp.where(eye, a, 0.0), axis=0, keepdims=True)

    def upright(a):
        return jnp.transpose(jnp.broadcast_to(a, (HD, HD)))

    def part(total, most):
        weight_sum = jnp.maximum(total[:, HD:], 1e-30)
        return (total[:, :HD] / weight_sum).astype(BF16), most * SCALE + jnp.log2(weight_sum)

    def join(total, most, other, level):
        level_own = most * SCALE
        high = jnp.maximum(level_own, level)
        own, far = jnp.exp2(level_own - high), jnp.exp2(level - high)
        return (total[:, :HD] * own + other.astype(F32) * far) / (total[:, HD:] * own + far)

    out, level = part(dacc[rows:], dtop[rows:])
    db[0] = out
    dst[0] = jnp.broadcast_to(flat(level), (8, HD))
    swaps[5].start()
    swaps[6].start()
    swaps[5].wait_recv()
    swaps[6].wait_recv()
    mixed = join(dacc[0:rows], dtop[0:rows], db[1], upright(dst[1, 0:1])).astype(BF16)
    for h in range(GROUP):
        att[z, h // 4, h % 4] = mixed[h * lines:(h + 1) * lines]

    def share(d, s, zb):
        return move(att.at[zb], att.at[zb], at_s.at[d, s - 1], at_r.at[d, s - 1], toward(d))

    def share_half(d, zb):
        ref = att.at[zb, d]
        return move(ref, ref, at_s.at[d, half - 1], at_r.at[d, half - 1], toward(d))

    for d in (0, 1):
        share(d, 1, z).start()

    def send_parts():
        @pl.when(xh == 0)
        def _():
            attend(1, z, False)

        @pl.when(z >= half)
        def _():
            attend(1, block(0, half), False)

        for pair in range(pairs):
            out, level = part(acc[pairs + pair], top[pairs + pair])
            ob[0, pair] = out
            for n in (0, 1):
                ost[0, 2 * pair + n:2 * pair + n + 1] = flat(level[n * tokens:(n + 1) * tokens])
        swaps[3].start()
        swaps[4].start()

    def pass_on(s, _):
        for d in (0, 1):
            zb = block(d, s)
            share(d, s, zb).wait_recv()

            @pl.when(s < half - 1)
            def _():
                share(d, s + 1, zb).start()

            @pl.when(s == half - 1)
            def _():
                share_half(d, zb).start()

        attend_number(half - 3 + s)

        @pl.when(s == early + 1)
        def _():
            send_parts()

        return 0

    lax.fori_loop(1, half, pass_on, 0)
    attend_number(2 * half - 3)
    weight_in(0, xh, 1 - c).wait_recv()
    weight_in(2, 1 - xh, 1 - c).wait_recv()
    loads[10].wait()
    for d in (0, 1):
        share_half(d, block(d, half)).wait_recv()

    lhs = jnp.concatenate(
        [att[:, h // 4, h % 4].reshape(nz * lines, HD) for h in range(GROUP)], axis=1
    )
    depth = sbuf.shape[2]
    for xx in (0, 1):
        term = dot(lhs, jnp.concatenate([wv[xx, 0], wv[xx, 1]], axis=1)).astype(BF16)
        for cc in (0, 1):
            for j in range(ntp):
                sbuf[j, xx * 2 + cc] = term[j * depth:(j + 1) * depth, cc * HD:(cc + 1) * HD]

    def deal(o, to, source):
        return move(
            sbuf.at[to // 4, to % 4],
            rbuf.at[source // 4, source % 4],
            rs.at[o - 1],
            rr.at[o - 1],
            (z * 4 + to % 4, to // 4),
        )

    def deal_out(o, _):
        deal(o, lax.rem(here + o, plane), here).start()
        return 0

    lax.fori_loop(1, plane, deal_out, 0)
    rbuf[tp, mine] = sbuf[tp, mine]

    @pl.when(z >= half)
    def _():
        attend(0, block(0, half), False)

    swaps[3].wait_recv()
    swaps[4].wait_recv()
    for pair in range(pairs):
        level = jnp.concatenate(
            [upright(ost[1, 2 * pair + n:2 * pair + n + 1]) for n in (0, 1)], axis=0
        )
        out = join(acc[pair], top[pair], ob[1, pair], level).astype(BF16)
        for n in (0, 1):
            first = (2 * pair + n) * HD
            prev[:, first:first + HD] = out[n * tokens:(n + 1) * tokens]
    store_pre = pltpu.make_async_copy(prev, pre_hbm, loc.at[11])
    store_pre.start()

    def deal_in(o, _):
        deal(o, lax.rem(here + o, plane), lax.rem(here + plane - o, plane)).wait_recv()
        return 0

    lax.fori_loop(1, plane, deal_in, 0)
    for n in range(4):
        total = rbuf[0, n].astype(F32)
        for j in range(1, ntp):
            total += rbuf[j, n].astype(F32)
        total = total.astype(BF16)
        for zz in range(depth // lines):
            first = (zz * 4 + n) * lines
            decv[first:first + lines] = total[zz * lines:(zz + 1) * lines]
    store_dec = pltpu.make_async_copy(decv, dec_hbm, loc.at[12])
    store_dec.start()

    def ring_sent(s, _):
        for p, d in every:
            along(d, p, s, block(d, s - 1)).wait_send()
        for d in (0, 1):
            over(d, s, c).wait_send()
            share(d, s, block(d, s - 1)).wait_send()
        return 0

    lax.fori_loop(1, half, ring_sent, 0)
    for d in (0, 1):
        along(d, d, half, block(d, half - 1)).wait_send()
        share_half(d, block(d, half - 1)).wait_send()
    over(0, half, c).wait_send()
    over_own(c).wait_send()
    for copy in swaps + weights_out:
        copy.wait_send()

    def dealt(o, _):
        deal(o, lax.rem(here + o, plane), here).wait_send()
        return 0

    lax.fori_loop(1, plane, dealt, 0)
    store_pre.wait()
    store_dec.wait()


def local(pre_q, pre_k, pre_v, page_table, dec_q, dec_new_k, dec_new_v, cache_k, cache_v, cache_len, out_weight):
    nz = lax.axis_size("ctx") // 4
    ntp = lax.axis_size("tp")
    half = nz // 2
    tokens, width = pre_q.shape
    row_dev, cache = cache_k.shape[:2]
    lines = row_dev * STEPS
    rows = GROUP * lines
    plane = 4 * ntp
    out_rows = nz * 4 * lines // ntp
    depth = nz // ntp * lines
    hbm = pl.BlockSpec(memory_space=pltpu.HBM)
    sem = pltpu.SemaphoreType.DMA

    def vmem(shape, dtype=BF16):
        return pltpu.VMEM(shape, dtype)

    return pl.pallas_call(
        functools.partial(kernel, nz, ntp),
        out_shape=(
            jax.ShapeDtypeStruct((tokens, width), BF16),
            jax.ShapeDtypeStruct((out_rows, HD), BF16),
        ),
        in_specs=[hbm] * 11,
        out_specs=(hbm, hbm),
        scratch_shapes=[
            pltpu.SMEM(page_table.shape, jnp.int32),
            pltpu.SMEM(cache_len.shape, jnp.int32),
            vmem(dec_q.shape),
            vmem(dec_new_k.shape),
            vmem(dec_new_v.shape),
            vmem((nz, 2, 2, tokens, HD)),
            vmem((2, tokens, width)),
            vmem((row_dev, cache, HD)),
            vmem((row_dev, cache, HD)),
            vmem((2, 2, width, HD)),
            vmem((GROUP, 2 * tokens, 2 * HD), F32),
            vmem((GROUP, 2 * tokens, HD), F32),
            vmem((lines, width), F32),
            vmem((HD, HD), F32),
            vmem((HD, HD), F32),
            vmem((2, rows, HD)),
            vmem((2, -(-nz // 8) * 8, HD), F32),
            vmem((2, nz, 8, 2 * tokens), F32),
            vmem((2 * rows, 2 * HD), F32),
            vmem((2 * rows, HD), F32),
            vmem((2, GROUP // 2, 2 * tokens, HD)),
            vmem((2, GROUP, HD), F32),
            vmem((2, rows, HD)),
            vmem((2, 8, HD), F32),
            vmem((nz, 2, 4, lines, HD)),
            vmem((ntp, 4, depth, HD)),
            vmem((ntp, 4, depth, HD)),
            vmem((tokens, width)),
            vmem((out_rows, HD)),
            sem((13,)),
            sem((2, 2, half)), sem((2, 2, half)),
            sem((2, half)), sem((2, half)),
            sem(()), sem(()),
            sem((7,)), sem((7,)),
            sem((3,)), sem((3,)),
            sem((2, half)), sem((2, half)),
            sem((plane - 1,)), sem((plane - 1,)),
        ],
        compiler_params=pltpu.CompilerParams(
            collective_id=0, has_side_effects=True, vmem_limit_bytes=63 << 20
        ),
    )(
        pre_q, pre_k, pre_v, page_table, dec_q, dec_new_k, dec_new_v, cache_k, cache_v, cache_len, out_weight
    )


def solution(mesh):
    placed = (
        P("ctx", "tp"),
        P("ctx", "tp"),
        P("ctx", "tp"),
        P("ctx", None),
        P("ctx", None, "tp"),
        P("ctx", None, "tp"),
        P("ctx", None, "tp"),
        P("ctx", None, "tp"),
        P("ctx", None, "tp"),
        P("ctx"),
        P("tp", "ctx"),
    )
    return jax.shard_map(
        local,
        mesh=mesh,
        in_specs=placed,
        out_specs=(P("ctx", "tp"), P("tp", "ctx")),
        check_vma=False,
    )
```

time: 96.5 us -> 83.3 us (0.86)
  local copies, waits for them, and re-layouts: 9.6 us -> 2.29 us
  Pallas kernels: 85.7 us -> 80.2 us
    unnamed x24 -> x4, local copies, waits for them, and re-layouts: 9.6 us -> 2.29 us
    pallas_call x1, Pallas kernels: 85.7 us -> 80.2 us  [local(): pl.pallas_call(functools.partial(kernel, nz, ntp), out_shape=(jax.ShapeDt...]
where the time goes in v2:
time: 83.3 us; the launch traced here: 83.1 us
  Pallas kernels  80.2 us (96%)
  local copies, waits for them, and re-layouts  2.29 us (3%)
    pallas_call x1, Pallas kernels, local(): pl.pallas_call(functools.partial(kernel, nz, ntp), out_shape=(jax.ShapeDt...  80.2 us
    unnamed x4, local copies, waits for them, and re-layouts  2.29 us

profile of v2, /device:TPU:1, one launch (start us, length us, event | category | flops | bytes accessed | tf_op | source)
XLA Modules:
  0.0 83.1 jit_solution(8259472938158778863)
XLA Ops:
  0.6 80.2 %shard_map.122 = (bf16[128,1024]{1,0:T(8,128)(2,1)}, bf16[128,128]{1,0:T(8,128)(2,1)}) custom-call(bf16[128,1024]{1,0:T(8,128)(2,1)} %q_hbm.1, bf16[128,128]{1,0:T(8,128)(2,1)} %k_hbm.1, bf16[128,128]{1,0:T(8,128)(2,1)} %v_hbm.1, s32[1,96]{1,0:T(1,128)} %table_hbm.1, bf16[4,4,1024]{2,1,0:T(4,128)(2,1)} %dq_hbm.1, bf16[4,4,128]{2,1,0:T(4,128)(2,1)} %nk_hbm.1, ...), custom_call_target="tpu_custom_call" | custom-call | tf_op jit(solution)/shard_map/pallas_call | solution.py:539
  80.8 0.0 copy-start
  80.8 1.7 %copy.15 = bf16[128,1024]{1,0:T(8,128)(2,1)} copy(bf16[128,1024]{1,0:T(8,128)(2,1)} %get-tuple-element.4) | data formatting | bytes 524288
  82.5 0.0 copy-done
  82.5 0.6 copy.16
Async XLA Ops:
  80.8 1.7 %copy-start = (bf16[128,128]{1,0:T(8,128)(2,1)S(1)}, bf16[128,128]{1,0:T(8,128)(2,1)}, u32[]{:S(2)}) copy-start(bf16[128,128]{1,0:T(8,128)(2,1)} %get-tuple-element.5) | copy-start | bytes 98308

commit v3 on v2

v3 whole, which is shorter than its diff:
```python
import functools
import math

import jax
import jax.numpy as jnp
from jax import lax
from jax.experimental import pallas as pl
from jax.experimental.pallas import tpu as pltpu
from jax.sharding import PartitionSpec as P

MESH = pl.DeviceIdType.MESH
HD = 128
GROUP = 8
STEPS = 4
EXTRA = 16
NEGATIVE = -1e30
SCALE = HD ** -0.5 * math.log2(math.e)
F32 = jnp.float32
BF16 = jnp.bfloat16


def dot_t(a, b):
    return lax.dot_general(a, b, (((1,), (1,)), ((), ())), preferred_element_type=F32)


def dot(a, b):
    return jnp.dot(a, b, preferred_element_type=F32)


def wide(a, n):
    return jnp.concatenate([a] * n, axis=1)


def with_ones(values):
    return jnp.concatenate([values, jnp.ones(values.shape, BF16)], axis=1)


def row_max(scores):
    top = jnp.max(scores, axis=1, keepdims=True)
    return jnp.broadcast_to(top, (scores.shape[0], HD))


def kernel(
    nz, ntp,
    q_hbm, k_hbm, v_hbm, table_hbm, dq_hbm, nk_hbm, nv_hbm, ck_hbm, cv_hbm, lens_hbm, w_hbm,
    pre_hbm, dec_hbm,
    lens, tab_in, v_in, q_in, dq_in, nk_in, nv_in,
    kv, qt, ck, cv, wv, acc, top, dq32, nk32, nv32, dqs, dqt, tabs, bias, dacc, dtop,
    ob, ost, db, dst, att, sbuf, rbuf, mbuf, fbuf, prev, decv,
    loc, zs, zr, ss, sr, os, orr, xs, xr, ws, wr, at_s, at_r, rs, rr, bs, br,
):
    half = nz // 2
    rounds = half // 2
    ctx = lax.axis_index("ctx")
    tp = lax.axis_index("tp")
    z, xh, c = ctx // 4, (ctx // 2) % 2, ctx % 2
    mine = ctx % 4
    tokens = q_in.shape[0]
    cache = ck.shape[1]
    slots = tab_in.shape[1]
    lines = dq32.shape[0]
    rows = GROUP * lines

    def turned(a):
        return jnp.transpose(a.astype(F32))

    def device(zz, xx, cc):
        return (zz * 4 + xx * 2 + cc, tp)

    def move(src, dst, send, recv, to):
        return pltpu.make_async_remote_copy(
            src_ref=src, dst_ref=dst, send_sem=send, recv_sem=recv, device_id=to, device_id_type=MESH
        )

    sibling = device(z, xh, 1 - c)
    beside = device(z, 1 - xh, c)
    across = device(z, 1 - xh, 1 - c)

    def toward(d, hops):
        return device(lax.rem(z + (hops if d == 0 else nz - hops), nz), xh, c)

    def block(d, s):
        return lax.rem(jnp.where(d == 0, z + nz - s, z + s), nz)

    loads = [
        pltpu.make_async_copy(a, b, loc.at[n])
        for n, (a, b) in enumerate((
            (k_hbm, kv.at[z, c, 0]),
            (v_hbm, v_in),
            (table_hbm, tab_in),
            (dq_hbm, dq_in),
            (nk_hbm, nk_in),
            (nv_hbm, nv_in),
            (lens_hbm, lens),
            (ck_hbm, ck),
            (cv_hbm, cv),
            (q_hbm, q_in),
            (w_hbm, wv.at[xh, c]),
        ))
    ]
    for load in loads:
        load.start()
    barrier = pltpu.get_barrier_semaphore()

    def greet(o, _):
        pl.semaphore_signal(barrier, inc=1, device_id=(ctx, lax.rem(tp + o, ntp)), device_id_type=MESH)
        return 0

    along_z = [toward(d, hops) for hops in (1, 2, 3) for d in (0, 1)]
    for to in along_z + [sibling, beside, across]:
        pl.semaphore_signal(barrier, inc=1, device_id=to, device_id_type=MESH)
    lax.fori_loop(1, ntp, greet, 0)
    loads[0].wait()
    loads[1].wait()
    kv[z, c, 1] = turned(v_in[...]).astype(BF16)
    pl.semaphore_wait(barrier, ntp + 8)

    def along(d, p, s, zb):
        ref = kv.at[zb, c, p]
        to = toward(d, 2 - s % 2)
        return move(ref, ref, zs.at[d, p, s - 1], zr.at[d, p, s - 1], to)

    def over(d, s, cc):
        ref = kv.at[block(d, s), cc]
        return move(ref, ref, ss.at[d, s - 1], sr.at[d, s - 1], sibling)

    def over_own(cc):
        ref = kv.at[z, cc]
        return move(ref, ref, os, orr, sibling)

    every = [(p, d) for p in (0, 1) for d in (0, 1)]
    for p, d in every:
        if rounds > 1 or p == d:
            along(d, p, 2, z).start()
    for p, d in every:
        along(d, p, 1, z).start()
    over_own(c).start()

    for load in loads[2:4]:
        load.wait()
    tabs[0] = jnp.full(tabs.shape[1:], -1, jnp.int32)
    tabs[0, 0:1, 0:slots] = tab_in[...]
    for r in range(4):
        dq32[pl.ds(r * STEPS, STEPS), :] = dq_in[r].astype(F32)
    line = dq32[...]
    stacked = jnp.concatenate([line[:, h * HD:(h + 1) * HD] for h in range(GROUP)], axis=0)
    dqs[...] = stacked.astype(BF16)
    dqt[0] = jnp.transpose(stacked).astype(BF16)

    def swap(n, src, dst):
        return move(src, dst, xs.at[n], xr.at[n], beside)

    swaps = [
        swap(0, dqt.at[0], dqt.at[1]),
        swap(1, tabs.at[0], tabs.at[1]),
        swap(2, qt.at[0], qt.at[1]),
        swap(3, ob.at[0], ob.at[1]),
        swap(4, ost.at[0], ost.at[1]),
        swap(5, db.at[0], db.at[1]),
        swap(6, dst.at[0], dst.at[1]),
    ]

    def weight(n, xx, source, to):
        return move(source, wv.at[xx, c], ws.at[n], wr.at[n], to)

    weights_out = [
        weight(0, xh, w_hbm, sibling),
        weight(1, xh, w_hbm, beside),
        weight(2, 1 - xh, wv.at[1 - xh, c], sibling),
    ]

    def weight_in(n, xx, cc):
        ref = wv.at[xx, cc]
        return move(ref, ref, ws.at[n], wr.at[n], sibling)

    for n in range(2):
        swaps[n].start()
    loads[9].wait()
    for h in range(GROUP):
        qt[0, :, h * HD:(h + 1) * HD] = turned(q_in[:, h * HD:(h + 1) * HD]).astype(BF16)
    swaps[2].start()
    for n in range(2):
        weights_out[n].start()

    def own_decode():
        for load in loads[4:9]:
            load.wait()
        nk32[...] = jnp.zeros_like(nk32)
        nv32[...] = jnp.zeros_like(nv32)
        for r in range(4):
            nk32[pl.ds(r * STEPS, STEPS), :] = nk_in[r].astype(F32)
            nv32[pl.ds(r * STEPS, STEPS), :] = nv_in[r].astype(F32)
        queries = dqs[...]
        q_id = lax.broadcasted_iota(jnp.int32, (rows, cache), 0)
        k_id = lax.broadcasted_iota(jnp.int32, (rows, cache), 1)
        q_row = (q_id >> 2) & 3
        scores = []
        for r in range(4):
            live = (q_row == r) & (k_id < lens[r])
            scores.append(jnp.where(live, dot_t(queries, ck[r]), NEGATIVE))
        n_id = lax.broadcasted_iota(jnp.int32, (rows, HD), 0)
        u_id = lax.broadcasted_iota(jnp.int32, (rows, HD), 1)
        live = ((u_id >> 2) == ((n_id >> 2) & 3)) & ((u_id & 3) <= (n_id & 3))
        scores.append(jnp.where(live, dot_t(queries, nk32[...].astype(BF16)), NEGATIVE))
        most = row_max(scores[-1])
        for r in range(4):
            most = jnp.maximum(most, row_max(scores[r]))
        total = jnp.zeros((rows, 2 * HD), F32)
        for r in range(4):
            weights = jnp.exp2((scores[r] - wide(most, cache // HD)) * SCALE)
            total += dot(weights.astype(BF16), with_ones(cv[r]))
        weights = jnp.exp2((scores[-1] - most) * SCALE)
        total += dot(weights.astype(BF16), with_ones(nv32[...].astype(BF16)))
        dacc[0:HD, 0:rows] = jnp.transpose(total[:, :HD])
        dacc[HD:, 0:rows] = jnp.transpose(total[:, HD:])[0:EXTRA]
        dtop[0:1, 0:rows] = jnp.transpose(most)[0:1]
        dacc[:, rows:] = jnp.zeros((HD + EXTRA, rows), F32)
        dtop[0:1, rows:] = jnp.full((1, rows), NEGATIVE, F32)

    def page_bias():
        line_id = lax.broadcasted_iota(jnp.int32, (nz * 16, HD), 0)
        page = (line_id >> 4) * 32 + xh * 16 + (line_id & 15)
        for n in (0, 1):
            named = jnp.where(page == tabs[n, 0:1], 1.0, 0.0)
            found = jnp.max(named, axis=1, keepdims=True)
            penalty = jnp.broadcast_to(jnp.where(found > 0.5, 0.0, NEGATIVE), (nz * 16, HD))
            bias[:, :, n * HD:(n + 1) * HD] = penalty.reshape(nz, 16, HD)

    def keys_of(blocks):
        return jnp.concatenate([kv[zb, cc, 0] for zb in blocks for cc in (0, 1)], axis=0)

    def values_of(blocks):
        values = jnp.concatenate([kv[zb, cc, 1] for zb in blocks for cc in (0, 1)], axis=1)
        return jnp.concatenate([values, jnp.ones((EXTRA, values.shape[1]), BF16)], axis=0)

    def update(scores, old, total, values):
        most = jnp.max(scores, axis=0, keepdims=True)
        if old is not None:
            most = jnp.maximum(old, most)
        weights = jnp.exp2((scores - most) * SCALE).astype(BF16)
        mixed = dot(values, weights)
        if old is not None:
            mixed += total * jnp.exp2((old - most) * SCALE)
        return most, mixed

    def decode_step(blocks):
        queries = jnp.concatenate([dqt[0], dqt[1]], axis=1)
        scores = dot(keys_of(blocks), queries)
        penalty = []
        for zb in blocks:
            lines_of = bias[zb]
            penalty += [jnp.broadcast_to(lines_of[n:n + 1], (16, 2 * rows)) for n in range(16)]
        scores = scores + jnp.concatenate(penalty, axis=0)
        most, mixed = update(scores, dtop[0:1], dacc[...], values_of(blocks))
        dacc[...] = mixed
        dtop[0:1] = most

    lanes = [slice(n, n + 2 * HD) for n in range(0, GROUP * HD, 2 * HD)]

    def attend(side, blocks, masked):
        keys = keys_of(blocks)
        values = values_of(blocks)
        scores = [dot(keys, qt[side, :, cols]) for cols in lanes]
        if masked:
            k_id = lax.broadcasted_iota(jnp.int32, (2 * tokens, 2 * HD), 0)
            q_id = lax.broadcasted_iota(jnp.int32, (2 * tokens, 2 * HD), 1) & (tokens - 1)
            live = k_id <= c * tokens + q_id
            done = [
                update(jnp.where(live, part_scores, NEGATIVE), None, None, values)
                for part_scores in scores
            ]
        else:
            done = [
                update(part_scores, top[side, 0:1, cols], acc[side, :, cols], values)
                for part_scores, cols in zip(scores, lanes)
            ]
        for (most, mixed), cols in zip(done, lanes):
            acc[side, :, cols] = mixed
            top[side, 0:1, cols] = most

    def attend_some(side, first, second, one, both):
        @pl.when(both)
        def _():
            attend(side, [first, second], False)

        @pl.when(one & jnp.logical_not(both))
        def _():
            attend(side, [first], False)

    early = 3 if half >= 8 else 0

    def numbered(n):
        side = jnp.where((n >= early) & (n < early + half - 1), 1, 0)
        s = jnp.where(n < early, n + 1, jnp.where(side == 1, n - early + 1, n - half + 2))
        return side, block(0, s), block(1, s), z >= s, z + s >= nz

    total_pairs = 2 * (half - 1)
    first_partner = early // 2 + 2

    def attend_range(start, stop):
        def one(n, _):
            attend_some(*numbered(n))
            return 0

        lax.fori_loop(start, stop, one, 0)

    own_decode()
    over_own(1 - c).wait_recv()
    attend(0, [z], True)
    acc[1] = jnp.zeros(acc.shape[1:], F32)
    top[1, 0:1] = jnp.full((1, GROUP * HD), NEGATIVE, F32)
    swaps[0].wait_recv()
    swaps[1].wait_recv()
    page_bias()
    decode_step([z])

    def ring(k, _):
        for p, d in every:
            zb = block(d, 2 * k - 2)
            along(d, p, 2 * k - 2, zb).wait_recv()
            if p == d:
                along(d, p, 2 * k, zb).start()
            else:
                @pl.when(k < rounds)
                def _():
                    along(d, p, 2 * k, zb).start()
        for p, d in every:
            along(d, p, 2 * k - 1, block(d, 2 * k - 2)).start()
        for d in (0, 1):
            over(d, 2 * k - 2, c).start()
        for p, d in every:
            along(d, p, 2 * k - 3, block(d, 2 * k - 3)).wait_recv()
        for d in (0, 1):
            over(d, 2 * k - 3, c).start()
        for s in (2 * k - 2, 2 * k - 3):
            for d in (0, 1):
                over(d, s, 1 - c).wait_recv()
        decode_step([block(d, s) for s in (2 * k - 3, 2 * k - 2) for d in (0, 1)])

        @pl.when(k == first_partner)
        def _():
            swaps[2].wait_recv()

        attend_range(2 * k - 4, 2 * k - 2)
        return 0

    lax.fori_loop(2, rounds + 1, ring, 0)
    if rounds < first_partner:
        swaps[2].wait_recv()
    weights_out[1].wait_recv()
    weights_out[2].start()
    for d in (0, 1):
        along(d, d, half, block(d, half)).wait_recv()
    over(0, half, c).start()
    for p, d in every:
        along(d, p, half - 1, block(d, half - 1)).wait_recv()
    for d in (0, 1):
        over(d, half - 1, c).start()
    over(0, half, 1 - c).wait_recv()
    for d in (0, 1):
        over(d, half - 1, 1 - c).wait_recv()
    decode_step([block(0, half - 1), block(1, half - 1), block(0, half)])

    def part(total, most):
        weight_sum = jnp.maximum(total[HD:HD + 1], 1e-30)
        return (total[:HD] / weight_sum).astype(BF16), most * SCALE + jnp.log2(weight_sum)

    def join(total, most, other, level):
        level_own = most * SCALE
        high = jnp.maximum(level_own, level)
        own, far = jnp.exp2(level_own - high), jnp.exp2(level - high)
        scale = 1.0 / (total[HD:HD + 1] * own + far)
        return total[:HD] * (own * scale) + other.astype(F32) * (far * scale)

    out, level = part(dacc[:, rows:], dtop[0:1, rows:])
    db[0] = out
    dst[0] = jnp.broadcast_to(level, (8, HD))
    swaps[5].start()
    swaps[6].start()
    done_pairs = 2 * (rounds - 1)
    attend_range(done_pairs, min(done_pairs + 2, total_pairs))
    done_pairs = min(done_pairs + 2, total_pairs)
    swaps[5].wait_recv()
    swaps[6].wait_recv()
    mixed = jnp.transpose(join(dacc[:, 0:rows], dtop[0:1, 0:rows], db[1], dst[1, 0:1])).astype(BF16)
    for h in range(GROUP):
        att[z, h // 4, h % 4] = mixed[h * lines:(h + 1) * lines]

    reach = 3

    def share(d, s, zb):
        ref = att.at[zb] if s < half else att.at[zb, d]
        to = toward(d, (s - 1) % reach + 1)
        return move(ref, ref, at_s.at[d, s - 1], at_r.at[d, s - 1], to)

    def spread(base):
        for s in range(min(base + reach, half), base, -1):
            for d in (0, 1):
                share(d, s, block(d, base)).start()

    def send_parts():
        def more(j, _):
            first = jnp.where(j == 0, z, block(0, half))
            attend_some(1, first, first, jnp.where(j == 0, 1 - xh, z // half) > 0, j < 0)
            return 0

        lax.fori_loop(0, 2, more, 0)
        out, level = part(acc[1], top[1, 0:1])
        ob[0] = out
        ost[0] = jnp.broadcast_to(level, (8, GROUP * HD))
        swaps[3].start()
        swaps[4].start()

    bases = list(range(0, half, reach))
    for base in bases:
        if base:
            for d in (0, 1):
                share(d, base, block(d, base)).wait_recv()
        spread(base)
        stop = total_pairs if base == bases[-1] else min(done_pairs + 2, total_pairs)
        if done_pairs < stop:
            attend_range(done_pairs, stop)
        done_pairs = stop
        if base == 0:
            send_parts()
    weight_in(0, xh, 1 - c).wait_recv()
    weight_in(2, 1 - xh, 1 - c).wait_recv()
    loads[10].wait()
    for s in range(1, half + 1):
        if s not in bases:
            for d in (0, 1):
                share(d, s, block(d, s)).wait_recv()

    lhs = jnp.concatenate(
        [att[:, h // 4, h % 4].reshape(nz * lines, HD) for h in range(GROUP)], axis=1
    )
    depth = sbuf.shape[2]
    for xx in (0, 1):
        term = dot(lhs, jnp.concatenate([wv[xx, 0], wv[xx, 1]], axis=1)).astype(BF16)
        for cc in (0, 1):
            for j in range(ntp):
                sbuf[j, xx * 2 + cc] = term[j * depth:(j + 1) * depth, cc * HD:(cc + 1) * HD]

    def deal(o, to, source):
        return move(sbuf.at[to], rbuf.at[source], rs.at[o - 1], rr.at[o - 1], (ctx, to))

    def deal_out(o, _):
        deal(o, lax.rem(tp + o, ntp), tp).start()
        return 0

    lax.fori_loop(1, ntp, deal_out, 0)
    rbuf[tp] = sbuf[tp]

    def deal_in(o, _):
        deal(o, lax.rem(tp + o, ntp), lax.rem(tp + ntp - o, ntp)).wait_recv()
        return 0

    lax.fori_loop(1, ntp, deal_in, 0)
    total = rbuf[0].astype(F32)
    for j in range(1, ntp):
        total += rbuf[j].astype(F32)
    mbuf[...] = total.astype(BF16)
    near = ((sibling, xh, 1 - c), (beside, 1 - xh, c), (across, 1 - xh, 1 - c))

    def hand(n):
        to, xx, cc = near[n]
        return move(mbuf.at[xx * 2 + cc], fbuf.at[mine], bs.at[n], br.at[n], to)

    def handed(n):
        to, xx, cc = near[n]
        return move(mbuf.at[mine], fbuf.at[xx * 2 + cc], bs.at[n], br.at[n], to)

    for n in range(3):
        hand(n).start()
    fbuf[mine] = mbuf[mine]

    @pl.when(z >= half)
    def _():
        attend(0, [block(0, half)], False)

    swaps[3].wait_recv()
    swaps[4].wait_recv()
    whole = join(acc[0], top[0, 0:1], ob[1], ost[1, 0:1])
    for h in range(GROUP):
        prev[:, h * HD:(h + 1) * HD] = jnp.transpose(whole[:, h * HD:(h + 1) * HD]).astype(BF16)
    store_pre = pltpu.make_async_copy(prev, pre_hbm, loc.at[11])
    store_pre.start()

    for n in range(3):
        handed(n).wait_recv()
    for n in range(4):
        for zz in range(depth // lines):
            first = (zz * 4 + n) * lines
            decv[first:first + lines] = fbuf[n, zz * lines:(zz + 1) * lines]
    store_dec = pltpu.make_async_copy(decv, dec_hbm, loc.at[12])
    store_dec.start()

    def ring_sent(s, _):
        for p, d in every:
            along(d, p, s, block(d, (s - 1) // 2 * 2)).wait_send()
        for d in (0, 1):
            over(d, s, c).wait_send()
        return 0

    lax.fori_loop(1, half, ring_sent, 0)
    for s in range(1, half + 1):
        for d in (0, 1):
            share(d, s, block(d, (s - 1) // reach * reach)).wait_send()
    for d in (0, 1):
        along(d, d, half, block(d, half - 2)).wait_send()
    over(0, half, c).wait_send()
    over_own(c).wait_send()
    for copy in swaps + weights_out:
        copy.wait_send()

    for n in range(3):
        hand(n).wait_send()

    def dealt(o, _):
        deal(o, lax.rem(tp + o, ntp), tp).wait_send()
        return 0

    lax.fori_loop(1, ntp, dealt, 0)
    store_pre.wait()
    store_dec.wait()


def local(pre_q, pre_k, pre_v, page_table, dec_q, dec_new_k, dec_new_v, cache_k, cache_v, cache_len, out_weight):
    nz = lax.axis_size("ctx") // 4
    ntp = lax.axis_size("tp")
    half = nz // 2
    tokens, width = pre_q.shape
    row_dev, cache = cache_k.shape[:2]
    lines = row_dev * STEPS
    rows = GROUP * lines
    out_rows = nz * 4 * lines // ntp
    depth = nz // ntp * lines
    hbm = pl.BlockSpec(memory_space=pltpu.HBM)
    sem = pltpu.SemaphoreType.DMA

    def vmem(shape, dtype=BF16):
        return pltpu.VMEM(shape, dtype)

    return pl.pallas_call(
        functools.partial(kernel, nz, ntp),
        out_shape=(
            jax.ShapeDtypeStruct((tokens, width), BF16),
            jax.ShapeDtypeStruct((out_rows, HD), BF16),
        ),
        in_specs=[hbm] * 11,
        out_specs=(hbm, hbm),
        scratch_shapes=[
            pltpu.SMEM(cache_len.shape, jnp.int32),
            vmem(page_table.shape, jnp.int32),
            vmem((tokens, HD)),
            vmem((tokens, width)),
            vmem(dec_q.shape),
            vmem(dec_new_k.shape),
            vmem(dec_new_v.shape),
            vmem((nz, 2, 2, tokens, HD)),
            vmem((2, HD, width)),
            vmem((row_dev, cache, HD)),
            vmem((row_dev, cache, HD)),
            vmem((2, 2, width, HD)),
            vmem((2, HD + EXTRA, width), F32),
            vmem((2, 8, width), F32),
            vmem((lines, width), F32),
            vmem((HD, HD), F32),
            vmem((HD, HD), F32),
            vmem((rows, HD)),
            vmem((2, HD, rows)),
            vmem((2, 8, HD), jnp.int32),
            vmem((nz, 16, 2 * rows), F32),
            vmem((HD + EXTRA, 2 * rows), F32),
            vmem((8, 2 * rows), F32),
            vmem((2, HD, width)),
            vmem((2, 8, width), F32),
            vmem((2, HD, rows)),
            vmem((2, 8, HD), F32),
            vmem((nz, 2, 4, lines, HD)),
            vmem((ntp, 4, depth, HD)),
            vmem((ntp, 4, depth, HD)),
            vmem((4, depth, HD)),
            vmem((4, depth, HD)),
            vmem((tokens, width)),
            vmem((out_rows, HD)),
            sem((13,)),
            sem((2, 2, half)), sem((2, 2, half)),
            sem((2, half)), sem((2, half)),
            sem(()), sem(()),
            sem((7,)), sem((7,)),
            sem((3,)), sem((3,)),
            sem((2, half)), sem((2, half)),
            sem((max(ntp - 1, 1),)), sem((max(ntp - 1, 1),)),
            sem((3,)), sem((3,)),
        ],
        compiler_params=pltpu.CompilerParams(
            collective_id=0, has_side_effects=True, vmem_limit_bytes=63 << 20
        ),
    )(
        pre_q, pre_k, pre_v, page_table, dec_q, dec_new_k, dec_new_v, cache_k, cache_v, cache_len, out_weight
    )


def solution(mesh):
    placed = (
        P("ctx", "tp"),
        P("ctx", "tp"),
        P("ctx", "tp"),
        P("ctx", None),
        P("ctx", None, "tp"),
        P("ctx", None, "tp"),
        P("ctx", None, "tp"),
        P("ctx", None, "tp"),
        P("ctx", None, "tp"),
        P("ctx"),
        P("tp", "ctx"),
    )
    return jax.shard_map(
        local,
        mesh=mesh,
        in_specs=placed,
        out_specs=(P("ctx", "tp"), P("tp", "ctx")),
        check_vma=False,
    )
```

time: 83.3 us -> 69.2 us (0.83)
  Pallas kernels: 80.2 us -> 66.1 us
    pallas_call x1, Pallas kernels: 80.2 us -> 66.1 us  [local(): pl.pallas_call(functools.partial(kernel, nz, ntp), out_shape=(jax.ShapeDt...]
where the time goes in v3:
time: 69.2 us; the launch traced here: 69.1 us
  Pallas kernels  66.1 us (96%)
  local copies, waits for them, and re-layouts  2.29 us (3%)
    pallas_call x1, Pallas kernels, local(): pl.pallas_call(functools.partial(kernel, nz, ntp), out_shape=(jax.ShapeDt...  66.1 us
    unnamed x4, local copies, waits for them, and re-layouts  2.29 us

profile of v3, /device:TPU:1, one launch (start us, length us, event | category | flops | bytes accessed | tf_op | source)
XLA Modules:
  0.0 69.1 jit_solution(16565810498214794193)
XLA Ops:
  0.6 66.1 %shard_map.122 = (bf16[128,1024]{1,0:T(8,128)(2,1)}, bf16[128,128]{1,0:T(8,128)(2,1)}) custom-call(bf16[128,1024]{1,0:T(8,128)(2,1)} %q_hbm.1, bf16[128,128]{1,0:T(8,128)(2,1)} %k_hbm.1, bf16[128,128]{1,0:T(8,128)(2,1)} %v_hbm.1, s32[1,96]{1,0:T(1,128)} %table_hbm.1, bf16[4,4,1024]{2,1,0:T(4,128)(2,1)} %dq_hbm.1, bf16[4,4,128]{2,1,0:T(4,128)(2,1)} %nk_hbm.1, ...), custom_call_target="tpu_custom_call" | custom-call | tf_op jit(solution)/shard_map/pallas_call | solution.py:544
  66.8 0.0 copy-start
  66.8 1.7 %copy.15 = bf16[128,1024]{1,0:T(8,128)(2,1)} copy(bf16[128,1024]{1,0:T(8,128)(2,1)} %get-tuple-element.4) | data formatting | bytes 524288
  68.5 0.0 copy-done
  68.5 0.6 copy.16
Async XLA Ops:
  66.8 1.7 %copy-start = (bf16[128,128]{1,0:T(8,128)(2,1)S(1)}, bf16[128,128]{1,0:T(8,128)(2,1)}, u32[]{:S(2)}) copy-start(bf16[128,128]{1,0:T(8,128)(2,1)} %get-tuple-element.5) | copy-start | bytes 98308

commit v4 on v3

--- a/solution.py
+++ b/solution.py
@@ -47,7 +47,7 @@
     lens, tab_in, v_in, q_in, dq_in, nk_in, nv_in,
     kv, qt, ck, cv, wv, acc, top, dq32, nk32, nv32, dqs, dqt, tabs, bias, dacc, dtop,
     ob, ost, db, dst, att, sbuf, rbuf, mbuf, fbuf, prev, decv,
-    loc, zs, zr, ss, sr, os, orr, xs, xr, ws, wr, at_s, at_r, rs, rr, bs, br,
+    loc, zs, zr, ss, sr, os, orr, xs, xr, ds, dr, js, jr, ws, wr, at_s, at_r, rs, rr, bs, br,
 ):
     half = nz // 2
     rounds = half // 2
@@ -75,6 +75,11 @@
     sibling = device(z, xh, 1 - c)
     beside = device(z, 1 - xh, c)
     across = device(z, 1 - xh, 1 - c)
+    near = (
+        (sibling, xh * 2 + 1 - c),
+        (beside, (1 - xh) * 2 + c),
+        (across, (1 - xh) * 2 + 1 - c),
+    )
 
     def toward(d, hops):
         return device(lax.rem(z + (hops if d == 0 else nz - hops), nz), xh, c)
@@ -138,27 +143,37 @@
 
     for load in loads[2:4]:
         load.wait()
-    tabs[0] = jnp.full(tabs.shape[1:], -1, jnp.int32)
-    tabs[0, 0:1, 0:slots] = tab_in[...]
+    tabs[mine] = jnp.full(tabs.shape[1:], -1, jnp.int32)
+    tabs[mine, 0:1, 0:slots] = tab_in[...]
     for r in range(4):
         dq32[pl.ds(r * STEPS, STEPS), :] = dq_in[r].astype(F32)
     line = dq32[...]
     stacked = jnp.concatenate([line[:, h * HD:(h + 1) * HD] for h in range(GROUP)], axis=0)
     dqs[...] = stacked.astype(BF16)
-    dqt[0] = jnp.transpose(stacked).astype(BF16)
+    dqt[mine] = jnp.transpose(stacked).astype(BF16)
 
     def swap(n, src, dst):
         return move(src, dst, xs.at[n], xr.at[n], beside)
 
     swaps = [
-        swap(0, dqt.at[0], dqt.at[1]),
-        swap(1, tabs.at[0], tabs.at[1]),
-        swap(2, qt.at[0], qt.at[1]),
-        swap(3, ob.at[0], ob.at[1]),
-        swap(4, ost.at[0], ost.at[1]),
-        swap(5, db.at[0], db.at[1]),
-        swap(6, dst.at[0], dst.at[1]),
+        swap(0, qt.at[0], qt.at[1]),
+        swap(1, ob.at[0], ob.at[1]),
+        swap(2, ost.at[0], ost.at[1]),
     ]
+
+    def tell(n, place):
+        to = near[n][0]
+        return [
+            move(ref.at[place], ref.at[place], ds.at[n, m], dr.at[n, m], to)
+            for m, ref in enumerate((dqt, tabs))
+        ]
+
+    def settle(n, source, target):
+        to = near[n][0]
+        return [
+            move(ref.at[0, source], ref.at[1, target], js.at[n, m], jr.at[n, m], to)
+            for m, ref in enumerate((db, dst))
+        ]
 
     def weight(n, xx, source, to):
         return move(source, wv.at[xx, c], ws.at[n], wr.at[n], to)
@@ -173,12 +188,13 @@
         ref = wv.at[xx, cc]
         return move(ref, ref, ws.at[n], wr.at[n], sibling)
 
-    for n in range(2):
-        swaps[n].start()
+    for n in range(3):
+        for copy in tell(n, mine):
+            copy.start()
     loads[9].wait()
     for h in range(GROUP):
         qt[0, :, h * HD:(h + 1) * HD] = turned(q_in[:, h * HD:(h + 1) * HD]).astype(BF16)
-    swaps[2].start()
+    swaps[0].start()
     for n in range(2):
         weights_out[n].start()
 
@@ -211,26 +227,30 @@
             total += dot(weights.astype(BF16), with_ones(cv[r]))
         weights = jnp.exp2((scores[-1] - most) * SCALE)
         total += dot(weights.astype(BF16), with_ones(nv32[...].astype(BF16)))
-        dacc[0:HD, 0:rows] = jnp.transpose(total[:, :HD])
-        dacc[HD:, 0:rows] = jnp.transpose(total[:, HD:])[0:EXTRA]
-        dtop[0:1, 0:rows] = jnp.transpose(most)[0:1]
-        dacc[:, rows:] = jnp.zeros((HD + EXTRA, rows), F32)
-        dtop[0:1, rows:] = jnp.full((1, rows), NEGATIVE, F32)
+        dacc[...] = jnp.zeros(dacc.shape, F32)
+        dtop[...] = jnp.full(dtop.shape, NEGATIVE, F32)
+        dacc[mine, 0:HD] = jnp.transpose(total[:, :HD])
+        dacc[mine, HD:] = jnp.transpose(total[:, HD:])[0:EXTRA]
+        dtop[mine, 0:1] = jnp.transpose(most)[0:1]
 
     def page_bias():
-        line_id = lax.broadcasted_iota(jnp.int32, (nz * 16, HD), 0)
-        page = (line_id >> 4) * 32 + xh * 16 + (line_id & 15)
-        for n in (0, 1):
+        line_id = lax.broadcasted_iota(jnp.int32, (nz * 8, HD), 0)
+        page = (line_id >> 3) * 32 + xh * 16 + c * 8 + (line_id & 7)
+        for n in range(4):
             named = jnp.where(page == tabs[n, 0:1], 1.0, 0.0)
             found = jnp.max(named, axis=1, keepdims=True)
-            penalty = jnp.broadcast_to(jnp.where(found > 0.5, 0.0, NEGATIVE), (nz * 16, HD))
-            bias[:, :, n * HD:(n + 1) * HD] = penalty.reshape(nz, 16, HD)
+            penalty = jnp.broadcast_to(jnp.where(found > 0.5, 0.0, NEGATIVE), (nz * 8, HD))
+            bias[:, :, n * HD:(n + 1) * HD] = penalty.reshape(nz, 8, HD)
 
     def keys_of(blocks):
         return jnp.concatenate([kv[zb, cc, 0] for zb in blocks for cc in (0, 1)], axis=0)
 
     def values_of(blocks):
-        values = jnp.concatenate([kv[zb, cc, 1] for zb in blocks for cc in (0, 1)], axis=1)
+        return with_ones_below(
+            jnp.concatenate([kv[zb, cc, 1] for zb in blocks for cc in (0, 1)], axis=1)
+        )
+
+    def with_ones_below(values):
         return jnp.concatenate([values, jnp.ones((EXTRA, values.shape[1]), BF16)], axis=0)
 
     def update(scores, old, total, values):
@@ -244,16 +264,20 @@
         return most, mixed
 
     def decode_step(blocks):
-        queries = jnp.concatenate([dqt[0], dqt[1]], axis=1)
-        scores = dot(keys_of(blocks), queries)
+        queries = jnp.concatenate([dqt[n] for n in range(4)], axis=1)
+        keys = jnp.concatenate([kv[zb, c, 0] for zb in blocks], axis=0)
+        values = with_ones_below(jnp.concatenate([kv[zb, c, 1] for zb in blocks], axis=1))
         penalty = []
         for zb in blocks:
             lines_of = bias[zb]
-            penalty += [jnp.broadcast_to(lines_of[n:n + 1], (16, 2 * rows)) for n in range(16)]
-        scores = scores + jnp.concatenate(penalty, axis=0)
-        most, mixed = update(scores, dtop[0:1], dacc[...], values_of(blocks))
-        dacc[...] = mixed
-        dtop[0:1] = most
+            penalty += [jnp.broadcast_to(lines_of[n:n + 1], (16, 4 * rows)) for n in range(8)]
+        scores = dot(keys, queries) + jnp.concatenate(penalty, axis=0)
+        old = jnp.concatenate([dtop[n, 0:1] for n in range(4)], axis=1)
+        total = jnp.concatenate([dacc[n] for n in range(4)], axis=1)
+        most, mixed = update(scores, old, total, values)
+        for n in range(4):
+            dacc[n] = mixed[:, n * rows:(n + 1) * rows]
+            dtop[n, 0:1] = most[:, n * rows:(n + 1) * rows]
 
     lanes = [slice(n, n + 2 * HD) for n in range(0, GROUP * HD, 2 * HD)]
 
@@ -287,15 +311,12 @@
         def _():
             attend(side, [first], False)
 
-    early = 3 if half >= 8 else 0
-
     def numbered(n):
-        side = jnp.where((n >= early) & (n < early + half - 1), 1, 0)
-        s = jnp.where(n < early, n + 1, jnp.where(side == 1, n - early + 1, n - half + 2))
+        side = jnp.where(n < half - 1, 1, 0)
+        s = jnp.where(side == 1, n + 1, n - half + 2)
         return side, block(0, s), block(1, s), z >= s, z + s >= nz
 
     total_pairs = 2 * (half - 1)
-    first_partner = early // 2 + 2
 
     def attend_range(start, stop):
         def one(n, _):
@@ -305,14 +326,21 @@
         lax.fori_loop(start, stop, one, 0)
 
     own_decode()
+    for n in range(3):
+        for copy in tell(n, near[n][1]):
+            copy.wait_recv()
+    page_bias()
+    decode_step([z])
     over_own(1 - c).wait_recv()
     attend(0, [z], True)
     acc[1] = jnp.zeros(acc.shape[1:], F32)
     top[1, 0:1] = jnp.full((1, GROUP * HD), NEGATIVE, F32)
-    swaps[0].wait_recv()
-    swaps[1].wait_recv()
-    page_bias()
-    decode_step([z])
+
+    def odd(s):
+        for p, d in every:
+            along(d, p, s, block(d, s)).wait_recv()
+        for d in (0, 1):
+            over(d, s, c).start()
 
     def ring(k, _):
         for p, d in every:
@@ -328,37 +356,25 @@
             along(d, p, 2 * k - 1, block(d, 2 * k - 2)).start()
         for d in (0, 1):
             over(d, 2 * k - 2, c).start()
-        for p, d in every:
-            along(d, p, 2 * k - 3, block(d, 2 * k - 3)).wait_recv()
-        for d in (0, 1):
-            over(d, 2 * k - 3, c).start()
-        for s in (2 * k - 2, 2 * k - 3):
-            for d in (0, 1):
-                over(d, s, 1 - c).wait_recv()
-        decode_step([block(d, s) for s in (2 * k - 3, 2 * k - 2) for d in (0, 1)])
-
-        @pl.when(k == first_partner)
+        decode_step([block(d, 2 * k - 2) for d in (0, 1)])
+
+        @pl.when(k > 2)
         def _():
-            swaps[2].wait_recv()
-
-        attend_range(2 * k - 4, 2 * k - 2)
+            odd(2 * k - 5)
+            decode_step([block(d, 2 * k - 5) for d in (0, 1)])
+
         return 0
 
     lax.fori_loop(2, rounds + 1, ring, 0)
-    if rounds < first_partner:
-        swaps[2].wait_recv()
     weights_out[1].wait_recv()
     weights_out[2].start()
+    if rounds > 1:
+        odd(half - 3)
+        decode_step([block(d, half - 3) for d in (0, 1)])
+    odd(half - 1)
     for d in (0, 1):
         along(d, d, half, block(d, half)).wait_recv()
     over(0, half, c).start()
-    for p, d in every:
-        along(d, p, half - 1, block(d, half - 1)).wait_recv()
-    for d in (0, 1):
-        over(d, half - 1, c).start()
-    over(0, half, 1 - c).wait_recv()
-    for d in (0, 1):
-        over(d, half - 1, 1 - c).wait_recv()
     decode_step([block(0, half - 1), block(1, half - 1), block(0, half)])
 
     def part(total, most):
@@ -372,17 +388,40 @@
         scale = 1.0 / (total[HD:HD + 1] * own + far)
         return total[:HD] * (own * scale) + other.astype(F32) * (far * scale)
 
-    out, level = part(dacc[:, rows:], dtop[0:1, rows:])
-    db[0] = out
-    dst[0] = jnp.broadcast_to(level, (8, HD))
-    swaps[5].start()
-    swaps[6].start()
-    done_pairs = 2 * (rounds - 1)
-    attend_range(done_pairs, min(done_pairs + 2, total_pairs))
-    done_pairs = min(done_pairs + 2, total_pairs)
-    swaps[5].wait_recv()
-    swaps[6].wait_recv()
-    mixed = jnp.transpose(join(dacc[:, 0:rows], dtop[0:1, 0:rows], db[1], dst[1, 0:1])).astype(BF16)
+    out, level = part(
+        jnp.concatenate([dacc[n] for n in range(4)], axis=1),
+        jnp.concatenate([dtop[n, 0:1] for n in range(4)], axis=1),
+    )
+    for n in range(4):
+        db[0, n] = out[:, n * rows:(n + 1) * rows]
+        dst[0, n] = jnp.broadcast_to(level[:, n * rows:(n + 1) * rows], (8, rows))
+    for n in range(3):
+        for copy in settle(n, near[n][1], mine):
+            copy.start()
+
+    def over_in(first, stop):
+        for s in range(first, stop):
+            for d in (0, 1):
+                over(d, s, 1 - c).wait_recv()
+
+    ready = min(3, half - 1)
+    swaps[0].wait_recv()
+    over_in(1, ready + 1)
+    attend_range(0, ready)
+    done_pairs = ready
+    for n in range(3):
+        for copy in settle(n, mine, near[n][1]):
+            copy.wait_recv()
+    levels = [dtop[mine, 0:1] * SCALE] + [dst[1, place, 0:1] for _, place in near]
+    high = functools.reduce(jnp.maximum, levels)
+    shares = [jnp.exp2(one - high) for one in levels]
+    own_part = dacc[mine]
+    mixed = own_part[:HD] * shares[0]
+    weight_sum = own_part[HD:HD + 1] * shares[0]
+    for (_, place), fraction in zip(near, shares[1:]):
+        mixed += db[1, place].astype(F32) * fraction
+        weight_sum += fraction
+    mixed = jnp.transpose(mixed / weight_sum).astype(BF16)
     for h in range(GROUP):
         att[z, h // 4, h % 4] = mixed[h * lines:(h + 1) * lines]
 
@@ -408,8 +447,8 @@
         out, level = part(acc[1], top[1, 0:1])
         ob[0] = out
         ost[0] = jnp.broadcast_to(level, (8, GROUP * HD))
-        swaps[3].start()
-        swaps[4].start()
+        swaps[1].start()
+        swaps[2].start()
 
     bases = list(range(0, half, reach))
     for base in bases:
@@ -417,12 +456,17 @@
             for d in (0, 1):
                 share(d, base, block(d, base)).wait_recv()
         spread(base)
-        stop = total_pairs if base == bases[-1] else min(done_pairs + 2, total_pairs)
-        if done_pairs < stop:
-            attend_range(done_pairs, stop)
-        done_pairs = stop
         if base == 0:
+            over_in(ready + 1, half)
+            over(0, half, 1 - c).wait_recv()
+            attend_range(done_pairs, half - 1)
+            done_pairs = half - 1
             send_parts()
+        if base == bases[-1]:
+            attend_range(done_pairs, total_pairs)
+        elif base:
+            attend_range(done_pairs, done_pairs + 4)
+            done_pairs += 4
     weight_in(0, xh, 1 - c).wait_recv()
     weight_in(2, 1 - xh, 1 - c).wait_recv()
     loads[10].wait()
@@ -460,15 +504,14 @@
     for j in range(1, ntp):
         total += rbuf[j].astype(F32)
     mbuf[...] = total.astype(BF16)
-    near = ((sibling, xh, 1 - c), (beside, 1 - xh, c), (across, 1 - xh, 1 - c))
 
     def hand(n):
-        to, xx, cc = near[n]
-        return move(mbuf.at[xx * 2 + cc], fbuf.at[mine], bs.at[n], br.at[n], to)
+        to, place = near[n]
+        return move(mbuf.at[place], fbuf.at[mine], bs.at[n], br.at[n], to)
 
     def handed(n):
-        to, xx, cc = near[n]
-        return move(mbuf.at[mine], fbuf.at[xx * 2 + cc], bs.at[n], br.at[n], to)
+        to, place = near[n]
+        return move(mbuf.at[mine], fbuf.at[place], bs.at[n], br.at[n], to)
 
     for n in range(3):
         hand(n).start()
@@ -478,8 +521,8 @@
     def _():
         attend(0, [block(0, half)], False)
 
-    swaps[3].wait_recv()
-    swaps[4].wait_recv()
+    swaps[1].wait_recv()
+    swaps[2].wait_recv()
     whole = join(acc[0], top[0, 0:1], ob[1], ost[1, 0:1])
     for h in range(GROUP):
         prev[:, h * HD:(h + 1) * HD] = jnp.transpose(whole[:, h * HD:(h + 1) * HD]).astype(BF16)
@@ -514,6 +557,8 @@
         copy.wait_send()
 
     for n in range(3):
+        for copy in tell(n, mine) + settle(n, near[n][1], mine):
+            copy.wait_send()
         hand(n).wait_send()
 
     def dealt(o, _):
@@ -568,15 +613,15 @@
             vmem((HD, HD), F32),
             vmem((HD, HD), F32),
             vmem((rows, HD)),
-            vmem((2, HD, rows)),
-            vmem((2, 8, HD), jnp.int32),
-            vmem((nz, 16, 2 * rows), F32),
-            vmem((HD + EXTRA, 2 * rows), F32),
-            vmem((8, 2 * rows), F32),
+            vmem((4, HD, rows)),
+            vmem((4, 8, HD), jnp.int32),
+            vmem((nz, 8, 4 * rows), F32),
+            vmem((4, HD + EXTRA, rows), F32),
+            vmem((4, 8, rows), F32),
             vmem((2, HD, width)),
             vmem((2, 8, width), F32),
-            vmem((2, HD, rows)),
-            vmem((2, 8, HD), F32),
+            vmem((2, 4, HD, rows)),
+            vmem((2, 4, 8, HD), F32),
             vmem((nz, 2, 4, lines, HD)),
             vmem((ntp, 4, depth, HD)),
             vmem((ntp, 4, depth, HD)),
@@ -588,7 +633,9 @@
             sem((2, 2, half)), sem((2, 2, half)),
             sem((2, half)), sem((2, half)),
             sem(()), sem(()),
-            sem((7,)), sem((7,)),
+            sem((3,)), sem((3,)),
+            sem((3, 2)), sem((3, 2)),
+            sem((3, 2)), sem((3, 2)),
             sem((3,)), sem((3,)),
             sem((2, half)), sem((2, half)),
             sem((max(ntp - 1, 1),)), sem((max(ntp - 1, 1),)),

time: 69.2 us -> 70.2 us (1.014)
  Pallas kernels: 66.1 us -> 67.1 us
    pallas_call x1, Pallas kernels: 66.1 us -> 67.1 us  [local(): pl.pallas_call(functools.partial(kernel, nz, ntp), out_shape=(jax.ShapeDt...]
where the time goes in v4:
time: 70.2 us; the launch traced here: 70 us
  Pallas kernels  67.1 us (96%)
  local copies, waits for them, and re-layouts  2.29 us (3%)
    pallas_call x1, Pallas kernels, local(): pl.pallas_call(functools.partial(kernel, nz, ntp), out_shape=(jax.ShapeDt...  67.1 us
    unnamed x4, local copies, waits for them, and re-layouts  2.29 us

profile of v4, /device:TPU:1, one launch (start us, length us, event | category | flops | bytes accessed | tf_op | source)
XLA Modules:
  0.0 70.0 jit_solution(17874594493070949792)
XLA Ops:
  0.6 67.1 %shard_map.122 = (bf16[128,1024]{1,0:T(8,128)(2,1)}, bf16[128,128]{1,0:T(8,128)(2,1)}) custom-call(bf16[128,1024]{1,0:T(8,128)(2,1)} %q_hbm.1, bf16[128,128]{1,0:T(8,128)(2,1)} %k_hbm.1, bf16[128,128]{1,0:T(8,128)(2,1)} %v_hbm.1, s32[1,96]{1,0:T(1,128)} %table_hbm.1, bf16[4,4,1024]{2,1,0:T(4,128)(2,1)} %dq_hbm.1, bf16[4,4,128]{2,1,0:T(4,128)(2,1)} %nk_hbm.1, ...), custom_call_target="tpu_custom_call" | custom-call | tf_op jit(solution)/shard_map/pallas_call | solution.py:589
  67.7 0.0 copy-start
  67.7 1.7 %copy.15 = bf16[128,1024]{1,0:T(8,128)(2,1)} copy(bf16[128,1024]{1,0:T(8,128)(2,1)} %get-tuple-element.4) | data formatting | bytes 524288
  69.4 0.0 copy-done
  69.4 0.6 copy.16
Async XLA Ops:
  67.7 1.7 %copy-start = (bf16[128,128]{1,0:T(8,128)(2,1)S(1)}, bf16[128,128]{1,0:T(8,128)(2,1)}, u32[]{:S(2)}) copy-start(bf16[128,128]{1,0:T(8,128)(2,1)} %get-tuple-element.5) | copy-start | bytes 98308

commit v5 on v4

--- a/solution.py
+++ b/solution.py
@@ -46,7 +46,7 @@
     pre_hbm, dec_hbm,
     lens, tab_in, v_in, q_in, dq_in, nk_in, nv_in,
     kv, qt, ck, cv, wv, acc, top, dq32, nk32, nv32, dqs, dqt, tabs, bias, dacc, dtop,
-    ob, ost, db, dst, att, sbuf, rbuf, mbuf, fbuf, prev, decv,
+    ob, ost, db, dst, att, sbuf, rbuf, mbuf, prev,
     loc, zs, zr, ss, sr, os, orr, xs, xr, ds, dr, js, jr, ws, wr, at_s, at_r, rs, rr, bs, br,
 ):
     half = nz // 2
@@ -103,8 +103,6 @@
             (w_hbm, wv.at[xh, c]),
         ))
     ]
-    for load in loads:
-        load.start()
     barrier = pltpu.get_barrier_semaphore()
 
     def greet(o, _):
@@ -114,16 +112,17 @@
     along_z = [toward(d, hops) for hops in (1, 2, 3) for d in (0, 1)]
     for to in along_z + [sibling, beside, across]:
         pl.semaphore_signal(barrier, inc=1, device_id=to, device_id_type=MESH)
+    for load in loads[:2]:
+        load.start()
     lax.fori_loop(1, ntp, greet, 0)
-    loads[0].wait()
-    loads[1].wait()
-    kv[z, c, 1] = turned(v_in[...]).astype(BF16)
+    for load in loads[2:]:
+        load.start()
     pl.semaphore_wait(barrier, ntp + 8)
 
-    def along(d, p, s, zb):
+    def along(d, p, s, zb, source=None):
         ref = kv.at[zb, c, p]
         to = toward(d, 2 - s % 2)
-        return move(ref, ref, zs.at[d, p, s - 1], zr.at[d, p, s - 1], to)
+        return move(ref if source is None else source, ref, zs.at[d, p, s - 1], zr.at[d, p, s - 1], to)
 
     def over(d, s, cc):
         ref = kv.at[block(d, s), cc]
@@ -134,11 +133,15 @@
         return move(ref, ref, os, orr, sibling)
 
     every = [(p, d) for p in (0, 1) for d in (0, 1)]
-    for p, d in every:
-        if rounds > 1 or p == d:
-            along(d, p, 2, z).start()
-    for p, d in every:
-        along(d, p, 1, z).start()
+    for p in (0, 1):
+        if p == 1:
+            loads[1].wait()
+            kv[z, c, 1] = turned(v_in[...]).astype(BF16)
+        for s in (2, 1):
+            for d in (0, 1):
+                if s == 1 or rounds > 1 or p == d:
+                    along(d, p, s, z, k_hbm if p == 0 else None).start()
+    loads[0].wait()
     over_own(c).start()
 
     for load in loads[2:4]:
@@ -313,10 +316,17 @@
 
     def numbered(n):
         side = jnp.where(n < half - 1, 1, 0)
-        s = jnp.where(side == 1, n + 1, n - half + 2)
+        return paired(side, jnp.where(side == 1, n + 1, 2 * (n - half + 1) + 1))
+
+    def paired(side, s):
         return side, block(0, s), block(1, s), z >= s, z + s >= nz
 
-    total_pairs = 2 * (half - 1)
+    def even(s):
+        for d in (0, 1):
+            over(d, s, 1 - c).wait_recv()
+        attend_some(*paired(0, s))
+
+    total_pairs = half - 1 + rounds
 
     def attend_range(start, stop):
         def one(n, _):
@@ -343,34 +353,34 @@
             over(d, s, c).start()
 
     def ring(k, _):
-        for p, d in every:
-            zb = block(d, 2 * k - 2)
-            along(d, p, 2 * k - 2, zb).wait_recv()
-            if p == d:
-                along(d, p, 2 * k, zb).start()
-            else:
-                @pl.when(k < rounds)
-                def _():
+        @pl.when(k <= rounds)
+        def _():
+            for p, d in every:
+                zb = block(d, 2 * k - 2)
+                along(d, p, 2 * k - 2, zb).wait_recv()
+                if p == d:
                     along(d, p, 2 * k, zb).start()
-        for p, d in every:
-            along(d, p, 2 * k - 1, block(d, 2 * k - 2)).start()
-        for d in (0, 1):
-            over(d, 2 * k - 2, c).start()
-        decode_step([block(d, 2 * k - 2) for d in (0, 1)])
+                else:
+                    @pl.when(k < rounds)
+                    def _():
+                        along(d, p, 2 * k, zb).start()
+            for p, d in every:
+                along(d, p, 2 * k - 1, block(d, 2 * k - 2)).start()
+            for d in (0, 1):
+                over(d, 2 * k - 2, c).start()
+            decode_step([block(d, 2 * k - 2) for d in (0, 1)])
 
         @pl.when(k > 2)
         def _():
             odd(2 * k - 5)
             decode_step([block(d, 2 * k - 5) for d in (0, 1)])
+            even(2 * k - 4)
 
         return 0
 
-    lax.fori_loop(2, rounds + 1, ring, 0)
+    lax.fori_loop(2, rounds + 2, ring, 0)
     weights_out[1].wait_recv()
     weights_out[2].start()
-    if rounds > 1:
-        odd(half - 3)
-        decode_step([block(d, half - 3) for d in (0, 1)])
     odd(half - 1)
     for d in (0, 1):
         along(d, d, half, block(d, half)).wait_recv()
@@ -400,11 +410,11 @@
             copy.start()
 
     def over_in(first, stop):
-        for s in range(first, stop):
+        for s in range(first | 1, stop, 2):
             for d in (0, 1):
                 over(d, s, 1 - c).wait_recv()
 
-    ready = min(3, half - 1)
+    ready = min(4, half - 1)
     swaps[0].wait_recv()
     over_in(1, ready + 1)
     attend_range(0, ready)
@@ -465,8 +475,8 @@
         if base == bases[-1]:
             attend_range(done_pairs, total_pairs)
         elif base:
-            attend_range(done_pairs, done_pairs + 4)
-            done_pairs += 4
+            attend_range(done_pairs, done_pairs + 2)
+            done_pairs += 2
     weight_in(0, xh, 1 - c).wait_recv()
     weight_in(2, 1 - xh, 1 - c).wait_recv()
     loads[10].wait()
@@ -503,19 +513,20 @@
     total = rbuf[0].astype(F32)
     for j in range(1, ntp):
         total += rbuf[j].astype(F32)
-    mbuf[...] = total.astype(BF16)
+    mbuf[...] = total.astype(BF16).reshape(mbuf.shape)
 
     def hand(n):
         to, place = near[n]
-        return move(mbuf.at[place], fbuf.at[mine], bs.at[n], br.at[n], to)
+        return move(mbuf.at[place], dec_hbm.at[:, mine], bs.at[n], br.at[n], to)
 
     def handed(n):
         to, place = near[n]
-        return move(mbuf.at[mine], fbuf.at[place], bs.at[n], br.at[n], to)
+        return move(mbuf.at[mine], dec_hbm.at[:, place], bs.at[n], br.at[n], to)
 
     for n in range(3):
         hand(n).start()
-    fbuf[mine] = mbuf[mine]
+    store_dec = pltpu.make_async_copy(mbuf.at[mine], dec_hbm.at[:, mine], loc.at[12])
+    store_dec.start()
 
     @pl.when(z >= half)
     def _():
@@ -531,12 +542,6 @@
 
     for n in range(3):
         handed(n).wait_recv()
-    for n in range(4):
-        for zz in range(depth // lines):
-            first = (zz * 4 + n) * lines
-            decv[first:first + lines] = fbuf[n, zz * lines:(zz + 1) * lines]
-    store_dec = pltpu.make_async_copy(decv, dec_hbm, loc.at[12])
-    store_dec.start()
 
     def ring_sent(s, _):
         for p, d in every:
@@ -586,11 +591,11 @@
     def vmem(shape, dtype=BF16):
         return pltpu.VMEM(shape, dtype)
 
-    return pl.pallas_call(
+    pre_out, dec_out = pl.pallas_call(
         functools.partial(kernel, nz, ntp),
         out_shape=(
             jax.ShapeDtypeStruct((tokens, width), BF16),
-            jax.ShapeDtypeStruct((out_rows, HD), BF16),
+            jax.ShapeDtypeStruct((depth // lines, 4, lines, HD), BF16),
         ),
         in_specs=[hbm] * 11,
         out_specs=(hbm, hbm),
@@ -625,10 +630,8 @@
             vmem((nz, 2, 4, lines, HD)),
             vmem((ntp, 4, depth, HD)),
             vmem((ntp, 4, depth, HD)),
-            vmem((4, depth, HD)),
-            vmem((4, depth, HD)),
+            vmem((4, depth // lines, lines, HD)),
             vmem((tokens, width)),
-            vmem((out_rows, HD)),
             sem((13,)),
             sem((2, 2, half)), sem((2, 2, half)),
             sem((2, half)), sem((2, half)),
@@ -647,6 +650,7 @@
     )(
         pre_q, pre_k, pre_v, page_table, dec_q, dec_new_k, dec_new_v, cache_k, cache_v, cache_len, out_weight
     )
+    return pre_out, dec_out.reshape(out_rows, HD)
 
 
 def solution(mesh):

time: 70.2 us -> 69.1 us (0.984)
  Pallas kernels: 67.1 us -> 66.1 us
    pallas_call x1, Pallas kernels: 67.1 us -> 66.1 us  [local(): pl.pallas_call(functools.partial(kernel, nz, ntp), out_shape=(jax.ShapeDt...]
where the time goes in v5:
time: 69.1 us; the launch traced here: 69 us
  Pallas kernels  66.1 us (96%)
  local copies, waits for them, and re-layouts  2.29 us (3%)
    pallas_call x1, Pallas kernels, local(): pl.pallas_call(functools.partial(kernel, nz, ntp), out_shape=(jax.ShapeDt...  66.1 us
    unnamed x4, local copies, waits for them, and re-layouts  2.29 us

profile of v5, /device:TPU:1, one launch (start us, length us, event | category | flops | bytes accessed | tf_op | source)
XLA Modules:
  0.0 69.0 jit_solution(12510639846661891837)
XLA Ops:
  0.6 66.1 %shard_map.122 = (bf16[128,1024]{1,0:T(8,128)(2,1)}, bf16[2,4,16,128]{3,2,1,0:T(8,128)(2,1)}) custom-call(bf16[128,1024]{1,0:T(8,128)(2,1)} %q_hbm.1, bf16[128,128]{1,0:T(8,128)(2,1)} %k_hbm.1, bf16[128,128]{1,0:T(8,128)(2,1)} %v_hbm.1, s32[1,96]{1,0:T(1,128)} %table_hbm.1, bf16[4,4,1024]{2,1,0:T(4,128)(2,1)} %dq_hbm.1, bf16[4,4,128]{2,1,0:T(4,128)(2,1)} %nk_hbm.1, ...), custom_call_target="tpu_custom_call" | custom-call | tf_op jit(solution)/shard_map/pallas_call | solution.py:594
  66.7 0.0 copy-start
  66.7 1.7 %copy.15 = bf16[128,1024]{1,0:T(8,128)(2,1)} copy(bf16[128,1024]{1,0:T(8,128)(2,1)} %get-tuple-element.8) | data formatting | bytes 524288
  68.4 0.0 copy-done
  68.4 0.6 copy.16
Async XLA Ops:
  66.7 1.7 %copy-start = (bf16[2,4,16,128]{3,2,1,0:T(8,128)(2,1)S(1)}, bf16[2,4,16,128]{3,2,1,0:T(8,128)(2,1)}, u32[]{:S(2)}) copy-start(bf16[2,4,16,128]{3,2,1,0:T(8,128)(2,1)} %get-tuple-element.5) | copy-start | bytes 98308

commit v6 on v5

--- a/solution.py
+++ b/solution.py
@@ -47,7 +47,7 @@
     lens, tab_in, v_in, q_in, dq_in, nk_in, nv_in,
     kv, qt, ck, cv, wv, acc, top, dq32, nk32, nv32, dqs, dqt, tabs, bias, dacc, dtop,
     ob, ost, db, dst, att, sbuf, rbuf, mbuf, prev,
-    loc, zs, zr, ss, sr, os, orr, xs, xr, ds, dr, js, jr, ws, wr, at_s, at_r, rs, rr, bs, br,
+    loc, zs, zr, ss, sr, os, orr, xs, xr, ds, dr, js, jr, ws, wr, vs, vr, at_s, at_r, rs, rr, bs, br,
 ):
     half = nz // 2
     rounds = half // 2
@@ -178,14 +178,16 @@
             for m, ref in enumerate((db, dst))
         ]
 
-    def weight(n, xx, source, to):
-        return move(source, wv.at[xx, c], ws.at[n], wr.at[n], to)
-
     weights_out = [
-        weight(0, xh, w_hbm, sibling),
-        weight(1, xh, w_hbm, beside),
-        weight(2, 1 - xh, wv.at[1 - xh, c], sibling),
+        move(w_hbm, wv.at[xh, c], ws.at[0], wr.at[0], sibling),
+        move(wv.at[1 - xh, c], wv.at[1 - xh, c], ws.at[1], wr.at[1], sibling),
     ]
+
+    def weight_half(n, xx):
+        lines_of = pl.ds(n * (wv.shape[2] // 2), wv.shape[2] // 2)
+        return move(
+            w_hbm.at[lines_of, :], wv.at[xx, c, lines_of, :], vs.at[n], vr.at[n], beside
+        )
 
     def weight_in(n, xx, cc):
         ref = wv.at[xx, cc]
@@ -198,8 +200,9 @@
     for h in range(GROUP):
         qt[0, :, h * HD:(h + 1) * HD] = turned(q_in[:, h * HD:(h + 1) * HD]).astype(BF16)
     swaps[0].start()
-    for n in range(2):
-        weights_out[n].start()
+    weights_out[0].start()
+    if rounds == 1:
+        weight_half(0, xh).start()
 
     def own_decode():
         for load in loads[4:9]:
@@ -368,6 +371,11 @@
                 along(d, p, 2 * k - 1, block(d, 2 * k - 2)).start()
             for d in (0, 1):
                 over(d, 2 * k - 2, c).start()
+
+            @pl.when(k == rounds)
+            def _():
+                weight_half(0, xh).start()
+
             decode_step([block(d, 2 * k - 2) for d in (0, 1)])
 
         @pl.when(k > 2)
@@ -379,8 +387,6 @@
         return 0
 
     lax.fori_loop(2, rounds + 2, ring, 0)
-    weights_out[1].wait_recv()
-    weights_out[2].start()
     odd(half - 1)
     for d in (0, 1):
         along(d, d, half, block(d, half)).wait_recv()
@@ -414,6 +420,7 @@
             for d in (0, 1):
                 over(d, s, 1 - c).wait_recv()
 
+    weight_half(1, xh).start()
     ready = min(4, half - 1)
     swaps[0].wait_recv()
     over_in(1, ready + 1)
@@ -466,6 +473,10 @@
             for d in (0, 1):
                 share(d, base, block(d, base)).wait_recv()
         spread(base)
+        if base == bases[min(1, len(bases) - 1)]:
+            for n in range(2):
+                weight_half(n, 1 - xh).wait_recv()
+            weights_out[1].start()
         if base == 0:
             over_in(ready + 1, half)
             over(0, half, 1 - c).wait_recv()
@@ -478,7 +489,7 @@
             attend_range(done_pairs, done_pairs + 2)
             done_pairs += 2
     weight_in(0, xh, 1 - c).wait_recv()
-    weight_in(2, 1 - xh, 1 - c).wait_recv()
+    weight_in(1, 1 - xh, 1 - c).wait_recv()
     loads[10].wait()
     for s in range(1, half + 1):
         if s not in bases:
@@ -558,7 +569,7 @@
         along(d, d, half, block(d, half - 2)).wait_send()
     over(0, half, c).wait_send()
     over_own(c).wait_send()
-    for copy in swaps + weights_out:
+    for copy in swaps + weights_out + [weight_half(n, xh) for n in range(2)]:
         copy.wait_send()
 
     for n in range(3):
@@ -639,7 +650,8 @@
             sem((3,)), sem((3,)),
             sem((3, 2)), sem((3, 2)),
             sem((3, 2)), sem((3, 2)),
-            sem((3,)), sem((3,)),
+            sem((2,)), sem((2,)),
+            sem((2,)), sem((2,)),
             sem((2, half)), sem((2, half)),
             sem((max(ntp - 1, 1),)), sem((max(ntp - 1, 1),)),
             sem((3,)), sem((3,)),

time: 69.1 us -> 70.3 us (1.017)
  Pallas kernels: 66.1 us -> 67.2 us
    pallas_call x1, Pallas kernels: 66.1 us -> 67.2 us  [local(): pl.pallas_call(functools.partial(kernel, nz, ntp), out_shape=(jax.ShapeDt...]
where the time goes in v6:
time: 70.3 us; the launch traced here: 70.2 us
  Pallas kernels  67.2 us (96%)
  local copies, waits for them, and re-layouts  2.29 us (3%)
    pallas_call x1, Pallas kernels, local(): pl.pallas_call(functools.partial(kernel, nz, ntp), out_shape=(jax.ShapeDt...  67.2 us
    unnamed x4, local copies, waits for them, and re-layouts  2.29 us

profile of v6, /device:TPU:1, one launch (start us, length us, event | category | flops | bytes accessed | tf_op | source)
XLA Modules:
  0.0 70.2 jit_solution(12758167008017419616)
XLA Ops:
  0.6 67.2 %shard_map.122 = (bf16[128,1024]{1,0:T(8,128)(2,1)}, bf16[2,4,16,128]{3,2,1,0:T(8,128)(2,1)}) custom-call(bf16[128,1024]{1,0:T(8,128)(2,1)} %q_hbm.1, bf16[128,128]{1,0:T(8,128)(2,1)} %k_hbm.1, bf16[128,128]{1,0:T(8,128)(2,1)} %v_hbm.1, s32[1,96]{1,0:T(1,128)} %table_hbm.1, bf16[4,4,1024]{2,1,0:T(4,128)(2,1)} %dq_hbm.1, bf16[4,4,128]{2,1,0:T(4,128)(2,1)} %nk_hbm.1, ...), custom_call_target="tpu_custom_call" | custom-call | tf_op jit(solution)/shard_map/pallas_call | solution.py:605
  67.9 0.0 copy-start
  67.9 1.7 %copy.15 = bf16[128,1024]{1,0:T(8,128)(2,1)} copy(bf16[128,1024]{1,0:T(8,128)(2,1)} %get-tuple-element.8) | data formatting | bytes 524288
  69.6 0.0 copy-done
  69.6 0.6 copy.16
Async XLA Ops:
  67.9 1.7 %copy-start = (bf16[2,4,16,128]{3,2,1,0:T(8,128)(2,1)S(1)}, bf16[2,4,16,128]{3,2,1,0:T(8,128)(2,1)}, u32[]{:S(2)}) copy-start(bf16[2,4,16,128]{3,2,1,0:T(8,128)(2,1)} %get-tuple-element.5) | copy-start | bytes 98308

commit v7 on v3

--- a/solution.py
+++ b/solution.py
@@ -46,7 +46,7 @@
     pre_hbm, dec_hbm,
     lens, tab_in, v_in, q_in, dq_in, nk_in, nv_in,
     kv, qt, ck, cv, wv, acc, top, dq32, nk32, nv32, dqs, dqt, tabs, bias, dacc, dtop,
-    ob, ost, db, dst, att, sbuf, rbuf, mbuf, fbuf, prev, decv,
+    ob, ost, db, dst, att, sbuf, rbuf, mbuf, prev,
     loc, zs, zr, ss, sr, os, orr, xs, xr, ws, wr, at_s, at_r, rs, rr, bs, br,
 ):
     half = nz // 2
@@ -98,8 +98,6 @@
             (w_hbm, wv.at[xh, c]),
         ))
     ]
-    for load in loads:
-        load.start()
     barrier = pltpu.get_barrier_semaphore()
 
     def greet(o, _):
@@ -109,16 +107,17 @@
     along_z = [toward(d, hops) for hops in (1, 2, 3) for d in (0, 1)]
     for to in along_z + [sibling, beside, across]:
         pl.semaphore_signal(barrier, inc=1, device_id=to, device_id_type=MESH)
+    for load in loads[:2]:
+        load.start()
     lax.fori_loop(1, ntp, greet, 0)
-    loads[0].wait()
-    loads[1].wait()
-    kv[z, c, 1] = turned(v_in[...]).astype(BF16)
+    for load in loads[2:]:
+        load.start()
     pl.semaphore_wait(barrier, ntp + 8)
 
-    def along(d, p, s, zb):
+    def along(d, p, s, zb, source=None):
         ref = kv.at[zb, c, p]
         to = toward(d, 2 - s % 2)
-        return move(ref, ref, zs.at[d, p, s - 1], zr.at[d, p, s - 1], to)
+        return move(ref if source is None else source, ref, zs.at[d, p, s - 1], zr.at[d, p, s - 1], to)
 
     def over(d, s, cc):
         ref = kv.at[block(d, s), cc]
@@ -129,11 +128,15 @@
         return move(ref, ref, os, orr, sibling)
 
     every = [(p, d) for p in (0, 1) for d in (0, 1)]
-    for p, d in every:
-        if rounds > 1 or p == d:
-            along(d, p, 2, z).start()
-    for p, d in every:
-        along(d, p, 1, z).start()
+    for p in (0, 1):
+        if p == 1:
+            loads[1].wait()
+            kv[z, c, 1] = turned(v_in[...]).astype(BF16)
+        for s in (2, 1):
+            for d in (0, 1):
+                if s == 1 or rounds > 1 or p == d:
+                    along(d, p, s, z, k_hbm if p == 0 else None).start()
+    loads[0].wait()
     over_own(c).start()
 
     for load in loads[2:4]:
@@ -459,20 +462,21 @@
     total = rbuf[0].astype(F32)
     for j in range(1, ntp):
         total += rbuf[j].astype(F32)
-    mbuf[...] = total.astype(BF16)
+    mbuf[...] = total.astype(BF16).reshape(mbuf.shape)
     near = ((sibling, xh, 1 - c), (beside, 1 - xh, c), (across, 1 - xh, 1 - c))
 
     def hand(n):
         to, xx, cc = near[n]
-        return move(mbuf.at[xx * 2 + cc], fbuf.at[mine], bs.at[n], br.at[n], to)
+        return move(mbuf.at[xx * 2 + cc], dec_hbm.at[:, mine], bs.at[n], br.at[n], to)
 
     def handed(n):
         to, xx, cc = near[n]
-        return move(mbuf.at[mine], fbuf.at[xx * 2 + cc], bs.at[n], br.at[n], to)
+        return move(mbuf.at[mine], dec_hbm.at[:, xx * 2 + cc], bs.at[n], br.at[n], to)
 
     for n in range(3):
         hand(n).start()
-    fbuf[mine] = mbuf[mine]
+    store_dec = pltpu.make_async_copy(mbuf.at[mine], dec_hbm.at[:, mine], loc.at[12])
+    store_dec.start()
 
     @pl.when(z >= half)
     def _():
@@ -488,12 +492,6 @@
 
     for n in range(3):
         handed(n).wait_recv()
-    for n in range(4):
-        for zz in range(depth // lines):
-            first = (zz * 4 + n) * lines
-            decv[first:first + lines] = fbuf[n, zz * lines:(zz + 1) * lines]
-    store_dec = pltpu.make_async_copy(decv, dec_hbm, loc.at[12])
-    store_dec.start()
 
     def ring_sent(s, _):
         for p, d in every:
@@ -541,11 +539,11 @@
     def vmem(shape, dtype=BF16):
         return pltpu.VMEM(shape, dtype)
 
-    return pl.pallas_call(
+    pre_out, dec_out = pl.pallas_call(
         functools.partial(kernel, nz, ntp),
         out_shape=(
             jax.ShapeDtypeStruct((tokens, width), BF16),
-            jax.ShapeDtypeStruct((out_rows, HD), BF16),
+            jax.ShapeDtypeStruct((depth // lines, 4, lines, HD), BF16),
         ),
         in_specs=[hbm] * 11,
         out_specs=(hbm, hbm),
@@ -580,10 +578,8 @@
             vmem((nz, 2, 4, lines, HD)),
             vmem((ntp, 4, depth, HD)),
             vmem((ntp, 4, depth, HD)),
-            vmem((4, depth, HD)),
-            vmem((4, depth, HD)),
+            vmem((4, depth // lines, lines, HD)),
             vmem((tokens, width)),
-            vmem((out_rows, HD)),
             sem((13,)),
             sem((2, 2, half)), sem((2, 2, half)),
             sem((2, half)), sem((2, half)),
@@ -600,6 +596,7 @@
     )(
         pre_q, pre_k, pre_v, page_table, dec_q, dec_new_k, dec_new_v, cache_k, cache_v, cache_len, out_weight
     )
+    return pre_out, dec_out.reshape(out_rows, HD)
 
 
 def solution(mesh):

time: 69.2 us -> 69.7 us (level)
  no operation moved by 1% of the time
where the time goes in v7:
time: 69.7 us; the launch traced here: 69.6 us
  Pallas kernels  66.6 us (96%)
  local copies, waits for them, and re-layouts  2.29 us (3%)
    pallas_call x1, Pallas kernels, local(): pl.pallas_call(functools.partial(kernel, nz, ntp), out_shape=(jax.ShapeDt...  66.6 us
    unnamed x4, local copies, waits for them, and re-layouts  2.29 us

profile of v7, /device:TPU:1, one launch (start us, length us, event | category | flops | bytes accessed | tf_op | source)
XLA Modules:
  0.0 69.6 jit_solution(12286572634228093992)
XLA Ops:
  0.6 66.6 %shard_map.122 = (bf16[128,1024]{1,0:T(8,128)(2,1)}, bf16[2,4,16,128]{3,2,1,0:T(8,128)(2,1)}) custom-call(bf16[128,1024]{1,0:T(8,128)(2,1)} %q_hbm.1, bf16[128,128]{1,0:T(8,128)(2,1)} %k_hbm.1, bf16[128,128]{1,0:T(8,128)(2,1)} %v_hbm.1, s32[1,96]{1,0:T(1,128)} %table_hbm.1, bf16[4,4,1024]{2,1,0:T(4,128)(2,1)} %dq_hbm.1, bf16[4,4,128]{2,1,0:T(4,128)(2,1)} %nk_hbm.1, ...), custom_call_target="tpu_custom_call" | custom-call | tf_op jit(solution)/shard_map/pallas_call | solution.py:542
  67.3 0.0 copy-start
  67.3 1.7 %copy.15 = bf16[128,1024]{1,0:T(8,128)(2,1)} copy(bf16[128,1024]{1,0:T(8,128)(2,1)} %get-tuple-element.8) | data formatting | bytes 524288
  69.0 0.0 copy-done
  69.0 0.6 copy.16
Async XLA Ops:
  67.3 1.7 %copy-start = (bf16[2,4,16,128]{3,2,1,0:T(8,128)(2,1)S(1)}, bf16[2,4,16,128]{3,2,1,0:T(8,128)(2,1)}, u32[]{:S(2)}) copy-start(bf16[2,4,16,128]{3,2,1,0:T(8,128)(2,1)} %get-tuple-element.5) | copy-start | bytes 98308
